TPU v7x, 32 devices: a whole 2x2x4 slice. The times are simulated.
32 devices in a mesh: band: 8 (over z, y), grid: 4 (over x, core).
Axes of the slice: x: 2, y: 2, z: 4, core: 2. Of those that a mesh axis runs over, the one named last changes fastest.
Arguments:
- orbitals: float32 [2, 16, 96, 9216], P(None, 'band', 'grid'), may hold values from -7 to 7
- local_potential: float32 [96, 9216], P('grid'), may hold values from 0.5 to 2
- plan: int32 [2], replicated, may hold values from 0 to 7, as said below
- occupancy: int32 [8], replicated, may hold values from 1 to 2, as said below
Outputs:
- new_orbitals: float32 [2, 16, 96, 9216], P(None, 'band', 'grid')
- energies: float32 [16], P('band')
Inputs may be any that keep to these rules, and one draw needn't show every extreme that they name: `plan`: distinct band groups, the last group among them. `occupancy`: some group has all 2 orbitals occupied and some group only one.
All inputs are finite; a program needn't handle non-finite values.
Results may differ from a plain program's by a relative error of at most 0.00016.
Values sent between devices are 32-bit elements; how exact they have to be, the bound alone decides.
A program may use at most 128 MiB of HBM per device.

v0:
```python
import math

import jax
import jax.numpy as jnp
from jax import lax
from jax.sharding import PartitionSpec as P

G = 96
ROUNDS = 2


TIME_STEP = 0.4
MIXING = 0.25
OMEGA = 0.106
BOX = 65.1


def spread(shard, axis, root):
    mine = lax.axis_index(axis) == root
    return lax.psum(jnp.where(mine, shard, jnp.zeros_like(shard)), axis)


def screened_kernel(freq_x, freq_y, freq_z):

    def fold(index):
        return jnp.where(index <= G // 2, index, index - G).astype(jnp.float32)

    step = 2.0 * math.pi / BOX
    reduce_first_axis = fold(freq_x)[:, None, None]
    fold_y = fold(freq_y)[None, :, None]
    folded_along_z = fold(freq_z)[None, None, :]
    wave = (
        step
        * step
        * (
            reduce_first_axis * reduce_first_axis
            + fold_y * fold_y
            + folded_along_z * folded_along_z
        )
    )
    safe = jnp.where(wave > 0, wave, jnp.float32(1.0))
    screen = -jnp.expm1(-wave / (4.0 * OMEGA * OMEGA)) / safe
    return jnp.where(wave > 0, screen, jnp.float32(1.0 / (4.0 * OMEGA * OMEGA)))


def hartley_matrix():
    index = jnp.arange(G, dtype=jnp.int32)
    product = index[:, None] * index[None, :] % G
    rotation_argument = product.astype(jnp.float32) * (2.0 * math.pi / G)
    return jnp.cos(rotation_argument) + jnp.sin(rotation_argument)


def mult(form, left, right):
    return jnp.einsum(form, left, right, precision=lax.Precision.HIGHEST)


def screened_solve(density, cosine_sine_transform):
    spectrum = mult("pxyz,zk->pxyk", density, cosine_sine_transform)
    spectrum = mult("pxyz,yk->pxkz", spectrum, cosine_sine_transform)
    every = jnp.arange(G, dtype=jnp.int32)
    block = lax.all_to_all(spectrum, "grid", split_axis=2, concat_axis=1, tiled=True)
    width = block.shape[2]
    global_y = lax.axis_index("grid") * width + jnp.arange(width, dtype=jnp.int32)
    kernel = screened_kernel(every, global_y, every)
    moved = mult("pxyz,xk->pkyz", block, cosine_sine_transform) * kernel
    moved = mult("pxyz,xk->pkyz", moved, cosine_sine_transform)
    field = lax.all_to_all(moved, "grid", split_axis=1, concat_axis=2, tiled=True)
    field = mult("pxyz,yk->pxkz", field, cosine_sine_transform)
    field = mult("pxyz,zk->pxyk", field, cosine_sine_transform)
    return field * (1.0 / (G * G * G))


def exchange_terms(section, source, weight, cosine_sine_transform):
    count_own = section.shape[1]
    count_src = source.shape[1]
    height = section.shape[2]
    own = section[:, :, None]
    other = source[:, None]
    dens_re = other[0] * own[0] + other[1] * own[1]
    dens_im = other[0] * own[1] - other[1] * own[0]
    density = jnp.stack([dens_re, dens_im]).reshape(2 * count_own * count_src, height, G, G)
    solved = screened_solve(density, cosine_sine_transform).reshape(
        2, count_own, count_src, height, G * G
    )
    wide = weight[None, :, None, None]
    term_re = jnp.sum(wide * (other[0] * solved[0] - other[1] * solved[1]), axis=1)
    term_im = jnp.sum(wide * (other[0] * solved[1] + other[1] * solved[0]), axis=1)
    return -MIXING * jnp.stack([term_re, term_im])


def per_device(orbitals, local_potential, plan, occupancy):
    count_own = orbitals.shape[1]
    k_first = jnp.stack([local_potential * orbitals[1], -local_potential * orbitals[0]])
    section = orbitals + TIME_STEP * k_first
    cosine_sine_transform = hartley_matrix()
    group_count = jnp.arange(occupancy.shape[0], dtype=jnp.int32)
    exchange = jnp.zeros_like(section)
    for turn in range(ROUNDS):
        source_group = plan[turn]
        filled = jnp.sum(jnp.where(group_count == source_group, occupancy, 0))
        weight = jnp.where(jnp.arange(count_own, dtype=jnp.int32) < filled, 2.0, 0.0).astype(
            jnp.float32
        )
        source = spread(section, "band", source_group)
        source, weight = (source, weight)
        exchange = exchange + exchange_terms(section, source, weight, cosine_sine_transform)
    hamil = local_potential * section + exchange
    k_second = jnp.stack([hamil[1], -hamil[0]])
    delta = 0.5 * TIME_STEP * (k_first + k_second)
    along = jnp.sum(orbitals * delta, axis=(0, 2, 3))
    squared_modulus = jnp.sum(delta * delta, axis=(0, 2, 3))
    energy = jnp.sum(section * hamil, axis=(0, 2, 3))
    along, squared_modulus, energy = lax.psum((along, squared_modulus, energy), "grid")
    factor = -2.0 * along / (squared_modulus + 1e-06)
    fresh = orbitals + factor[None, :, None, None] * delta
    own_filled = jnp.sum(jnp.where(group_count == lax.axis_index("band"), occupancy, 0))
    filling = jnp.where(jnp.arange(count_own, dtype=jnp.int32) < own_filled, 2.0, 0.0).astype(
        jnp.float32
    )
    return (fresh, filling * energy / (G * G * G))


def solution(mesh):
    return jax.shard_map(
        per_device,
        mesh=mesh,
        in_specs=(P(None, "band", "grid", None), P("grid", None), P(), P()),
        out_specs=(P(None, "band", "grid", None), P("band")),
        check_vma=False,
    )
```

profile of v0, /device:TPU:0, one launch (start us, length us, event | category | flops | bytes accessed | tf_op | source)
XLA Modules:
  0.0 828.0 jit_solution(7991468417977250610)
XLA Ops:
  22.0 234.8 %all-reduce.4.cloned.1.call-done = (f32[2,2,24,9216]{3,2,1,0:T(8,128)}, f32[2,2,24,9216]{3,2,1,0:T(8,128)}) async-done(((f32[2,2,24,9216]{3,2,1,0:T(8,128)}, f32[2,2,24,9216]{3,2,1,0:T(8,128)}), (f32[2,2,24,9216]{3,2,1,0:T(8,128)}, f32[2,2,24,9216]{3,2,1,0:T(8,128)})) %all-reduce.4.cloned.1.call-update) | async-done | bytes 7077904 | tf_op jit(solution)/shard_map/psum | solution.py:20
  268.2 9.3 %reshape.158 = f32[8,24,96,96]{3,2,1,0:T(8,128)} reshape(f32[2,2,2,24,9216]{4,3,2,1,0:T(8,128)} %pad_maximum_fusion) | data formatting | bytes 14155776 | tf_op jit(solution)/shard_map/reshape | solution.py:81
  277.6 11.2 %fusion.40 = f32[8,24,96,96]{3,2,1,0:T(8,128)S(1)} fusion(f32[8,24,96,96]{3,2,1,0:T(8,128)} %reshape.158), kind=kOutput, calls=%fused_computation.68 | convolution fusion | flops 2038523904 | bytes 14155776 | tf_op jit(solution)/shard_map/pxyz,zk->pxyk/dot_general | solution.py:54
  288.8 9.6 %convolution_bitcast_fusion.1 = f32[8,24,96,96]{3,2,1,0:T(8,128)S(1)} fusion(f32[8,24,96,96]{3,2,1,0:T(8,128)S(1)} %fusion.40), kind=kOutput, calls=%fused_computation.41 | convolution fusion | flops 2038523904 | bytes 14155776 | tf_op jit(solution)/shard_map/pxyz,yk->pxkz/dot_general | solution.py:54
  298.4 9.3 %copy.33 = f32[8,24,96,96]{3,1,0,2:T(8,128)} copy(f32[8,24,96,96]{3,2,1,0:T(8,128)S(1)} %convolution_bitcast_fusion.1) | data formatting | bytes 14155776 | tf_op jit(solution)/shard_map/pxyz,yk->pxkz/transpose | solution.py:54
  318.9 9.3 %reshape.159 = f32[8,24,96,96]{3,2,1,0:T(8,128)} reshape(f32[2,2,2,24,9216]{4,3,2,1,0:T(8,128)} %pad_maximum_fusion.1) | data formatting | bytes 14155776 | tf_op jit(solution)/shard_map/reshape | solution.py:81
  328.2 10.9 %fusion.37 = f32[8,24,96,96]{3,2,1,0:T(8,128)S(1)} fusion(f32[8,24,96,96]{3,2,1,0:T(8,128)} %reshape.159), kind=kOutput, calls=%fused_computation.65 | convolution fusion | flops 2038523904 | bytes 14155776 | tf_op jit(solution)/shard_map/pxyz,zk->pxyk/dot_general | solution.py:54
  339.1 9.6 %convolution_bitcast_fusion = f32[8,24,96,96]{3,2,1,0:T(8,128)S(1)} fusion(f32[8,24,96,96]{3,2,1,0:T(8,128)S(1)} %fusion.37), kind=kOutput, calls=%fused_computation.40 | convolution fusion | flops 2038523904 | bytes 14155776 | tf_op jit(solution)/shard_map/pxyz,yk->pxkz/dot_general | solution.py:54
  348.8 9.6 %copy.44 = f32[8,24,96,96]{3,1,0,2:T(8,128)} copy(f32[8,24,96,96]{3,2,1,0:T(8,128)S(1)} %convolution_bitcast_fusion) | data formatting | bytes 14155776 | tf_op jit(solution)/shard_map/pxyz,yk->pxkz/transpose | solution.py:54
  358.4 59.5 %all-to-all-done = f32[8,24,96,96]{3,1,0,2:T(8,128)} async-done(((f32[8,24,96,96]{3,1,0,2:T(8,128)}), f32[8,24,96,96]{3,1,0,2:T(8,128)}, u32[]{:S(2)}, u32[]{:S(2)}) %all-to-all-start) | async-done | bytes 7077920 | tf_op jit(solution)/shard_map/all_to_all | solution.py:61
  424.6 9.1 %copy.35 = f32[8,4,24,24,96]{4,3,2,1,0:T(8,128)S(1)} copy(f32[8,4,24,24,96]{4,2,0,3,1:T(8,128)} %bitcast.14) | data formatting | bytes 14155776 | tf_op jit(solution)/shard_map/all_to_all | solution.py:61
  433.7 10.2 %fusion.10 = f32[96,8,24,96]{3,0,2,1:T(8,128)S(1)} fusion(f32[8,96,24,96]{3,2,1,0:T(8,128)S(1)} %bitcast.115), kind=kOutput, calls=%fused_computation.10 | convolution fusion | flops 2038523904 | bytes 14155776 | tf_op jit(solution)/shard_map/pxyz,xk->pkyz/dot_general | solution.py:54
  443.9 10.2 %fusion.18 = f32[8,96,24,96]{3,1,2,0:T(8,128)S(1)} fusion(f32[96,8,24,96]{3,0,2,1:T(8,128)S(1)} %fusion.10, f32[96,24,96]{2,0,1:T(8,128)S(1)} %compare_select_fusion), kind=kOutput, calls=%fused_computation.38 | convolution fusion | flops 2040293376 | bytes 15040512 | tf_op jit(solution)/shard_map/pxyz,xk->pkyz/dot_general | solution.py:54
  454.1 9.1 %copy.39 = f32[8,96,24,96]{3,2,0,1:T(8,128)} copy(f32[8,96,24,96]{3,1,2,0:T(8,128)S(1)} %fusion.18) | data formatting | bytes 14155776 | tf_op jit(solution)/shard_map/pxyz,xk->pkyz/transpose | solution.py:54
  463.3 64.8 %all-to-all-done.2 = f32[8,24,96,96]{3,1,0,2:T(8,128)} async-done(((f32[8,24,96,96]{3,1,0,2:T(8,128)}), f32[8,24,96,96]{3,1,0,2:T(8,128)}, u32[]{:S(2)}, u32[]{:S(2)}) %all-to-all-start.2) | async-done | bytes 7077920 | tf_op jit(solution)/shard_map/all_to_all | solution.py:61
  534.3 9.1 %copy.46 = f32[8,4,24,24,96]{4,3,2,1,0:T(8,128)S(1)} copy(f32[8,4,24,24,96]{4,2,0,3,1:T(8,128)} %bitcast.36) | data formatting | bytes 14155776 | tf_op jit(solution)/shard_map/all_to_all | solution.py:61
  543.5 10.2 %fusion.8 = f32[96,8,24,96]{3,0,2,1:T(8,128)S(1)} fusion(f32[8,96,24,96]{3,2,1,0:T(8,128)S(1)} %bitcast.116), kind=kOutput, calls=%fused_computation.8 | convolution fusion | flops 2038523904 | bytes 14155776 | tf_op jit(solution)/shard_map/pxyz,xk->pkyz/dot_general | solution.py:54
  553.7 10.2 %fusion.23 = f32[8,96,24,96]{3,1,2,0:T(8,128)S(1)} fusion(f32[96,8,24,96]{3,0,2,1:T(8,128)S(1)} %fusion.8, f32[96,24,96]{2,0,1:T(8,128)S(1)} %compare_select_fusion), kind=kOutput, calls=%fused_computation.39 | convolution fusion | flops 2040293376 | bytes 15040512 | tf_op jit(solution)/shard_map/pxyz,xk->pkyz/dot_general | solution.py:54
  573.0 65.3 %all-to-all-done.1 = f32[8,96,24,96]{3,2,0,1:T(8,128)} async-done(((f32[8,96,24,96]{3,2,0,1:T(8,128)}), f32[8,96,24,96]{3,2,0,1:T(8,128)}, u32[]{:S(2)}, u32[]{:S(2)}) %all-to-all-start.1) | async-done | bytes 7077920 | tf_op jit(solution)/shard_map/all_to_all | solution.py:67
  652.5 9.6 %fusion.45 = f32[96,8,24,96]{3,0,2,1:T(8,128)S(1)} fusion(f32[8,24,96,96]{3,2,1,0:T(8,128)S(1)} %bitcast.117), kind=kOutput, calls=%fused_computation.73 | convolution fusion | flops 2038523904 | bytes 14155776 | tf_op jit(solution)/shard_map/pxyz,yk->pxkz/dot_general | solution.py:54
  662.1 9.4 %broadcast_multiply_fusion.1 = f32[8,24,96,96]{3,2,1,0:T(8,128)S(1)} fusion(f32[96,8,24,96]{3,0,2,1:T(8,128)S(1)} %fusion.45), kind=kOutput, calls=%fused_computation.17 | convolution fusion | flops 2040293376 | bytes 14155776 | tf_op jit(solution)/shard_map/pxyz,zk->pxyk/dot_general | solution.py:54
  688.4 60.1 %all-to-all-done.3 = f32[8,96,24,96]{3,2,0,1:T(8,128)} async-done(((f32[8,96,24,96]{3,2,0,1:T(8,128)}), f32[8,96,24,96]{3,2,0,1:T(8,128)}, u32[]{:S(2)}, u32[]{:S(2)}) %all-to-all-start.3) | async-done | bytes 7077920 | tf_op jit(solution)/shard_map/all_to_all | solution.py:67
  753.5 9.6 %fusion.34 = f32[96,8,24,96]{3,0,2,1:T(8,128)S(1)} fusion(f32[8,24,96,96]{3,2,1,0:T(8,128)S(1)} %bitcast.118), kind=kOutput, calls=%fused_computation.62 | convolution fusion | flops 2038523904 | bytes 14155776 | tf_op jit(solution)/shard_map/pxyz,yk->pxkz/dot_general | solution.py:54
  763.2 9.2 %broadcast_multiply_fusion = f32[8,24,96,96]{3,2,1,0:T(8,128)S(1)} fusion(f32[96,8,24,96]{3,0,2,1:T(8,128)S(1)} %fusion.34), kind=kOutput, calls=%fused_computation.16 | convolution fusion | flops 2040293376 | bytes 14155776 | tf_op jit(solution)/shard_map/pxyz,zk->pxyk/dot_general | solution.py:54
  (90 shorter events, 142.6 us)
Async XLA Ops:
  7.2 249.6 %all-reduce.4.cloned.1.call-start = ((), (), s32[]{:S(2)}) async-start(), calls=%async_computation.4 | async-start | bytes 14155776 | tf_op jit(solution)/shard_map/psum | solution.py:20
  11.1 3.3 copy-start
  256.7 3.9 copy-start.21
  256.7 4.1 copy-start.22
  260.6 4.0 copy-start.8
  260.7 4.0 copy-start.10
  260.7 4.0 copy-start.12
  260.7 4.0 copy-start.14
  307.7 110.2 %all-to-all-start = ((f32[8,24,96,96]{3,1,0,2:T(8,128)}), f32[8,24,96,96]{3,1,0,2:T(8,128)}, u32[]{:S(2)}, u32[]{:S(2)}) async-start(f32[8,24,96,96]{3,1,0,2:T(8,128)} %copy.33), calls=%async_computation | async-start | bytes 18874368 | tf_op jit(solution)/shard_map/all_to_all | solution.py:61
  417.9 110.2 %all-to-all-start.2 = ((f32[8,24,96,96]{3,1,0,2:T(8,128)}), f32[8,24,96,96]{3,1,0,2:T(8,128)}, u32[]{:S(2)}, u32[]{:S(2)}) async-start(f32[8,24,96,96]{3,1,0,2:T(8,128)} %copy.44), calls=%async_computation.2 | async-start | bytes 18874368 | tf_op jit(solution)/shard_map/all_to_all | solution.py:61
  528.1 110.2 %all-to-all-start.1 = ((f32[8,96,24,96]{3,2,0,1:T(8,128)}), f32[8,96,24,96]{3,2,0,1:T(8,128)}, u32[]{:S(2)}, u32[]{:S(2)}) async-start(f32[8,96,24,96]{3,2,0,1:T(8,128)} %copy.39), calls=%async_computation.1 | async-start | bytes 18874368 | tf_op jit(solution)/shard_map/all_to_all | solution.py:67
  573.0 71.1 %copy-start.24 = (s32[8]{0:T(128)S(1)}, s32[8]{0:T(128)}, u32[]{:S(2)}) copy-start(s32[8]{0:T(128)} %param.7) | copy-start | bytes 100
  638.3 110.2 %all-to-all-start.3 = ((f32[8,96,24,96]{3,2,0,1:T(8,128)}), f32[8,96,24,96]{3,2,0,1:T(8,128)}, u32[]{:S(2)}, u32[]{:S(2)}) async-start(f32[8,96,24,96]{3,2,0,1:T(8,128)} %copy.50), calls=%async_computation.3 | async-start | bytes 18874368 | tf_op jit(solution)/shard_map/all_to_all | solution.py:67
  783.0 6.2 copy-start.13
  783.0 6.2 copy-start.15
  789.2 6.5 copy-start.9
  789.2 6.5 copy-start.11
  789.2 6.4 copy-start.18
  789.2 6.4 copy-start.19
  795.7 3.4 copy-start.23
  801.6 3.8 copy-start.5
  801.6 4.4 copy-start.7
  801.9 5.6 copy-start.16
  801.9 5.6 copy-start.17
  (6 other events, 17.8 us)
Sparse Core Ops, SparseCore 0:
  19.5 237.2 all-reduce.3
where the time goes:
time: 835 us; the launch traced here: 828 us
  waiting for transfers between devices  485 us (58%)
  local copies, waits for them, and re-layouts  131 us (16%)
  matrix products  120 us (14%)
  other arithmetic  46.2 us (6%)
  starting transfers between devices  23.6 us (3%)
  between operations  15.9 us (2%)
    psum x1, waiting for transfers between devices, spread(): return lax.psum(jnp.where(mine, shard, jnp.zeros_like(shard)), axis)  235 us
    all_to_all x2, waiting for transfers between devices, screened_solve(): lax.all_to_all(moved, 'grid', split_axis=1, concat_axis=2, tiled=True)  125 us
    all_to_all x2, waiting for transfers between devices, screened_solve(): lax.all_to_all(spectrum, 'grid', split_axis=2, concat_axis=1, tiled=True)  124 us
    dot_general x12, matrix products, mult(): return jnp.einsum(form, left, right, precision=lax.Precision.HIGHEST)  120 us
    transpose x4, local copies, waits for them, and re-layouts, mult(): return jnp.einsum(form, left, right, precision=lax.Precision.HIGHEST)  37.2 us
    reshape x2, local copies, waits for them, and re-layouts, exchange_terms(): jnp.stack([dens_re, dens_im])  18.6 us
    all_to_all x2, local copies, waits for them, and re-layouts, screened_solve(): lax.all_to_all(spectrum, 'grid', split_axis=2, concat_axis=1, tiled=True)  18.3 us
  transfers between devices with their start and end apart: 5, of which 5 were waited for; matrix products, arithmetic and copies ran while one was open for 20% of the time, Pallas kernels for 0%

commit v1 on v0

v1 whole, which is shorter than its diff:
```python
import functools
import math

import jax
import jax.numpy as jnp
from jax import lax
from jax.experimental import pallas as pl
from jax.experimental.pallas import tpu as pltpu
from jax.sharding import PartitionSpec as P

MESH = pl.DeviceIdType.MESH
VMEM_BYTES = 56 * 1024 * 1024

TIME_STEP = 0.4
MIXING = 0.25
OMEGA = 0.106
BOX = 65.1


def screened_kernel(points, start, width):
    def square(index):
        fold = jnp.where(index <= points // 2, index, index - points).astype(jnp.float32)
        return fold * fold

    every = square(jnp.arange(points, dtype=jnp.int32))
    part = square(start + jnp.arange(width, dtype=jnp.int32))
    step = 2.0 * math.pi / BOX
    wave = step * step * (every[:, None, None] + part[None, :, None] + every[None, None, :])
    safe = jnp.where(wave > 0, wave, jnp.float32(1.0))
    screen = -jnp.expm1(-wave / (4.0 * OMEGA * OMEGA)) / safe
    return jnp.where(wave > 0, screen, jnp.float32(1.0 / (4.0 * OMEGA * OMEGA)))


def hartley_rows(rows, points):
    product = rows[:, None] * jnp.arange(points, dtype=jnp.int32)[None, :] % points
    angle = product.astype(jnp.float32) * (2.0 * math.pi / points)
    return jnp.cos(angle) + jnp.sin(angle)


def mult(form, left, right):
    return jnp.einsum(form, left, right, precision=lax.Precision.HIGH)


def ring_place(band, bands):
    half = lax.div(band, 2)
    odd = lax.rem(band, 2)
    return (1 - odd) * half + odd * (bands - 1 - half)


def gather_kernel(
    bands,
    plan,
    section,
    cross_out,
    side_out,
    side_cross_out,
    stream_out,
    side_stream_out,
    cross,
    landed,
    stream,
    cross_send,
    cross_recv,
    ring_send,
    ring_recv,
    side_send,
    side_recv,
    keep,
):
    chunks, width = cross.shape[0], cross.shape[-1]
    half = chunks // 2
    steps = landed.shape[1]
    band, here = lax.axis_index("band"), lax.axis_index("grid")
    place = ring_place(band, bands)

    def member(spot):
        back = lax.div(spot, bands // 2)
        return (1 - back) * 2 * spot + back * (2 * (bands - 1 - spot) + 1)

    ring = (
        {"band": member(lax.rem(place + 1, bands))},
        {"band": member(lax.rem(place + bands - 1, bands))},
    )
    partner = {"grid": lax.rem(here + 2, 4)}
    sibling = {"grid": here + 1 - 2 * lax.rem(here, 2)}

    barrier = pltpu.get_barrier_semaphore()
    for other in (*ring, partner, sibling):
        pl.semaphore_signal(barrier, inc=1, device_id=other, device_id_type=MESH)
    pl.semaphore_wait(barrier, 4)

    def remote(source, target, send, recv, device):
        return pltpu.make_async_remote_copy(
            src_ref=source,
            dst_ref=target,
            send_sem=send,
            recv_sem=recv,
            device_id=device,
            device_id_type=MESH,
        )

    def lanes(k):
        return pl.ds(pl.multiple_of(k * width, 128), width)

    def cross_copy(k):
        return remote(
            section.at[:, :, :, lanes(k)], cross.at[k], cross_send.at[k], cross_recv.at[k], partner
        )

    def ring_copy(way, t):
        return remote(
            stream.at[way, t],
            landed.at[way, t],
            ring_send.at[way, t],
            ring_recv.at[way, t],
            ring[way],
        )

    bounds = ((0, half), (half, half), (chunks, steps + 1 - chunks))

    def side_copy(k):
        if k == 0:
            source, target = section, side_out
        elif k == 1:
            source, target = cross, side_cross_out
        else:
            cut = pl.ds(*bounds[k - 2])
            source, target = stream.at[:, cut], side_stream_out.at[:, cut]
        return remote(source, target, side_send.at[k], side_recv.at[k], sibling)

    def keep_copy(k):
        if k == 0:
            return pltpu.make_async_copy(cross, cross_out, keep.at[k])
        cut = pl.ds(*bounds[k - 1])
        return pltpu.make_async_copy(stream.at[:, cut], stream_out.at[:, cut], keep.at[k])

    def store(part):
        side_copy(part + 2).start()
        keep_copy(part + 1).start()

    root = plan[lax.div(here, 2)]
    mine = jnp.full(stream.shape[2:], root, jnp.int32) == band

    @pl.loop(0, half)
    def _(k):
        cross_copy(k).start()
        cross_copy(half + k).start()

    for way in range(2):
        stream[way, 0] = section[:, :, :, way * half * width : (way * half + 1) * width]
        ring_copy(way, 0).start()
    side_copy(0).start()

    @pl.loop(1, half)
    def _(t):
        for way in range(2):
            ring_copy(way, t - 1).wait_recv()
            own = section[:, :, :, lanes(way * half + t)]
            stream[way, t] = jnp.where(mine, own, landed[way, t - 1])
            ring_copy(way, t).start()

    store(0)

    @pl.loop(half, chunks)
    def _(t):
        for way in range(2):
            k = way * half + t - half
            cross_copy(k).wait_recv()
            ring_copy(way, t - 1).wait_recv()
            stream[way, t] = jnp.where(mine, cross[k], landed[way, t - 1])
            ring_copy(way, t).start()

    store(1)
    side_copy(1).start()
    keep_copy(0).start()

    @pl.loop(chunks, steps)
    def _(t):
        for way in range(2):
            ring_copy(way, t - 1).wait_recv()
            stream[way, t] = landed[way, t - 1]
            ring_copy(way, t).start()

    for way in range(2):
        ring_copy(way, steps - 1).wait_recv()
        stream[way, steps] = landed[way, steps - 1]
    store(2)

    @pl.loop(0, chunks)
    def _(k):
        cross_copy(k).wait_send()

    @pl.loop(0, steps)
    def _(t):
        for way in range(2):
            ring_copy(way, t).wait_send()

    for k in range(5):
        side_copy(k).wait()
    for k in range(4):
        keep_copy(k).wait()


def gather(section, plan, bands, width):
    height, plane = section.shape[2], section.shape[3]
    chunks = plane // width
    steps = chunks + bands - 2
    piece = (2, 2, height, width)
    whole = jax.ShapeDtypeStruct((chunks, *piece), jnp.float32)
    log = jax.ShapeDtypeStruct((2, steps + 1, *piece), jnp.float32)
    dma = pltpu.SemaphoreType.DMA
    return pl.pallas_call(
        functools.partial(gather_kernel, bands),
        out_shape=(whole, jax.ShapeDtypeStruct(section.shape, jnp.float32), whole, log, log),
        in_specs=[
            pl.BlockSpec(memory_space=pltpu.SMEM),
            pl.BlockSpec(memory_space=pltpu.VMEM),
        ],
        out_specs=[pl.BlockSpec(memory_space=pl.ANY)] * 5,
        scratch_shapes=[
            pltpu.VMEM(whole.shape, jnp.float32),
            pltpu.VMEM((2, steps, *piece), jnp.float32),
            pltpu.VMEM(log.shape, jnp.float32),
            dma((chunks,)),
            dma((chunks,)),
            dma((2, steps)),
            dma((2, steps)),
            dma((5,)),
            dma((5,)),
            dma((4,)),
        ],
        compiler_params=pltpu.CompilerParams(
            collective_id=0, has_side_effects=True, vmem_limit_bytes=VMEM_BYTES
        ),
    )(plan, section)


def halves(value):
    high = value.astype(jnp.bfloat16)
    return high, (value - high.astype(jnp.float32)).astype(jnp.bfloat16)


def dot(left, right, axis=0):
    return lax.dot_general(
        left, right, (((1,), (axis,)), ((), ())), preferred_element_type=jnp.float32
    )


def three(left, right, axis=0):
    return dot(left[0], right[0], axis) + (dot(left[0], right[1], axis) + dot(left[1], right[0], axis))


def solve_kernel(
    points,
    info,
    weight,
    square_z,
    decay_z,
    s0,
    s1,
    s2,
    s3,
    o0,
    o1,
    o2,
    o3,
    zcut_high,
    zcut_low,
    z_high,
    z_low,
    x_high,
    x_low,
    y_pair,
    y_low,
    square_xy,
    decay_xy,
    near,
    far,
    work,
):
    phase, step = pl.program_id(0), pl.program_id(1)
    width = near.shape[-1]
    tiles = work.shape[0]
    window = zcut_high.shape[2]
    rows = pl.ds(pl.multiple_of(step * width, width), width)

    def source(part, j):
        return jnp.concatenate([s[0, 0, part, j] for s in (s0, s1, s2, s3)], axis=0)

    @pl.when(phase == 0)
    def _():
        own_re, own_im = (
            jnp.concatenate([o0[p, 0], o1[p, 0], o2[0, p, 0], o3[0, p, 0]], axis=0)
            for p in range(2)
        )
        fields = []
        for j in range(2):
            s_re, s_im = source(0, j), source(1, j)
            fields.append(s_re * own_re + s_im * own_im)
            fields.append(s_re * own_im - s_im * own_re)
        high, low = halves(jnp.concatenate(fields, axis=0))
        parts = []
        for k in range(2):
            cut = slice(k * (width - window), k * (width - window) + window)
            parts.append(
                three((zcut_high[k], zcut_low[k]), (high[:, cut], low[:, cut]), 1)
            )
        along = halves(jnp.concatenate(parts, axis=0))
        out = three(along, (x_high[...], x_low[...]))
        for k in range(tiles):
            work[k, rows, :] = out[:, 128 * k : 128 * (k + 1)]

    @pl.when(jnp.logical_and(phase == 0, step == pl.num_programs(1) - 1))
    def _():
        scale = 1.0 / (points * points * points)

        def across(value):
            high, low = halves(value)
            return dot(y_pair[...], jnp.concatenate([high, low], axis=0)) + dot(y_low[...], high)

        @pl.loop(0, points // 4)
        def _(group):
            for pair in range(2):
                first = group * 4 + pair * 2
                lines = [pl.ds(first + u, points, stride=points) for u in range(2)]
                value = jnp.concatenate(
                    [work[k, line, :] for line in lines for k in range(tiles)], axis=1
                )
                factors = []
                for u in range(2):
                    wave = square_xy[...] + square_z[first + u]
                    safe = jnp.where(wave > 0, wave, 1.0)
                    screen = (scale - decay_xy[...] * (decay_z[first + u] * scale)) / safe
                    factors.append(
                        jnp.where(wave > 0, screen, scale / (4.0 * OMEGA * OMEGA))
                    )
                value = across(across(value) * jnp.concatenate(factors, axis=1))
                for u in range(2):
                    for k in range(tiles):
                        at = 128 * (u * tiles + k)
                        work[k, lines[u], :] = value[:, at : at + 128]

    @pl.when(phase == 1)
    def _():
        spectrum = halves(jnp.concatenate([work[k, rows, :] for k in range(tiles)], axis=1))
        along = halves(three((x_high[...], x_low[...]), spectrum, 1))
        field = three(along, (z_high[...], z_low[...]))
        term_re = term_im = 0.0
        for j in range(2):
            v_re = field[2 * j * points : (2 * j + 1) * points]
            v_im = field[(2 * j + 1) * points : (2 * j + 2) * points]
            s_re, s_im = source(0, j), source(1, j)
            term_re = term_re + weight[j] * (s_re * v_re - s_im * v_im)
            term_im = term_im + weight[j] * (s_re * v_im + s_im * v_re)
        middle = points // 2
        for k, term in enumerate((term_re, term_im)):
            near[k] = term[:middle]
            far[k] = term[middle:]


def solve(section, gathered, plan, weights, along_x, bands, width):
    cross, side, side_cross, stream, side_stream = gathered
    height, plane = section.shape[2], section.shape[3]
    points = along_x.shape[0]
    chunks = plane // width
    half = chunks // 2
    here = lax.axis_index("grid")
    place = ring_place(lax.axis_index("band"), bands)
    root = ring_place(jnp.where(here // 2 == 0, plan[0], plan[1]), bands)
    info = jnp.stack(
        [lax.rem(place - root + bands, bands), lax.rem(root - place + bands, bands), here % 2]
    ).astype(jnp.int32)

    index = jnp.arange(points, dtype=jnp.int32)
    along = hartley_rows(index, points)
    four = jnp.eye(4, dtype=jnp.float32)

    def blocks(matrix):
        return jnp.einsum("ab,ij->aibj", four, matrix).reshape(width, width)

    def split(value):
        high = lax.reduce_precision(value, 8, 7)
        return high.astype(jnp.bfloat16), (value - high).astype(jnp.bfloat16)

    z_high, z_low = split(blocks(along))
    x_high, x_low = split(blocks(along_x))
    y_high, y_low = split(along)
    window = -(-(width // 2) // 128) * 128

    def cuts(matrix):
        return jnp.stack([matrix[: width // 2, :window], matrix[width // 2 :, width - window :]])

    fold = jnp.where(index <= points // 2, index, index - points).astype(jnp.float32)
    base = 2.0 * math.pi / BOX
    square = base * base * (fold * fold)
    decay = jnp.exp(-square / (4.0 * OMEGA * OMEGA))
    square_x, decay_x = jnp.tile(square, 4), jnp.tile(decay, 4)
    square_xy = square[:, None] + square_x[None, :]
    decay_xy = decay[:, None] * decay_x[None, :]
    tables = [
        cuts(z_high),
        cuts(z_low),
        z_high,
        z_low,
        x_high,
        x_low,
        jnp.concatenate([y_high, y_high], axis=1),
        y_low,
        square_xy,
        decay_xy,
    ]

    def line(offset):
        def spot(p, i, info):
            way = lax.div(i, half)
            return (way, info[way] + lax.rem(i, half) + offset, 0, 0, 0, 0)

        return pl.BlockSpec((1, 1, 2, 2, height, width), spot)

    natural = pl.BlockSpec(
        (2, 1, height, width), lambda p, i, info: (0, info[2], 0, (1 - p) * i + p * (chunks - 1))
    )
    piece = pl.BlockSpec(
        (1, 2, 1, height, width),
        lambda p, i, info: ((1 - p) * i + p * (chunks - 1), 0, info[2], 0, 0),
    )
    scalars = pl.BlockSpec(memory_space=pltpu.SMEM)
    result = pl.BlockSpec((2, 2 * height, width), lambda p, i, info: (0, 0, p * i))

    def full(table):
        return pl.BlockSpec(table.shape, lambda p, i, info: (0,) * table.ndim)

    half_grid = jax.ShapeDtypeStruct((2, 2 * height, plane), jnp.float32)
    return pl.pallas_call(
        functools.partial(solve_kernel, points),
        grid_spec=pltpu.PrefetchScalarGridSpec(
            num_scalar_prefetch=1,
            grid=(2, chunks),
            in_specs=[scalars] * 3
            + [line(0), line(0), line(half), line(half)]
            + [natural, natural, piece, piece]
            + [full(table) for table in tables],
            out_specs=[result, result],
            scratch_shapes=[pltpu.VMEM((width // 128, plane, 128), jnp.float32)],
        ),
        out_shape=(half_grid, half_grid),
        compiler_params=pltpu.CompilerParams(
            dimension_semantics=("arbitrary", "arbitrary"), vmem_limit_bytes=VMEM_BYTES
        ),
    )(
        info,
        weights,
        square,
        decay,
        stream,
        side_stream,
        stream,
        side_stream,
        section,
        side,
        cross,
        side_cross,
        *tables,
    )


def per_device(orbitals, local_potential, plan, occupancy):
    rounds = plan.shape[0]
    count_own = orbitals.shape[1]
    height = orbitals.shape[2]
    plane = orbitals.shape[3]
    points = math.isqrt(plane)
    devices = lax.axis_size("grid")
    parts = devices // 4
    here = lax.axis_index("grid")
    share, slot = here // parts, here % parts
    first_core, first_chip = share % 2 == 0, share // 2 == 0
    teams = [[q * parts + s for s in range(parts)] for q in range(4)]

    def swap(value, bit):
        return lax.ppermute(
            value, "grid", [(g, ((g // parts) ^ bit) * parts + g % parts) for g in range(devices)]
        )

    def core_swap(value):
        return swap(value, 1)

    def chip_swap(value):
        return swap(value, 2)

    def turn(value, split, concat):
        if parts == 1:
            return value
        return lax.all_to_all(
            value, "grid", split, concat, axis_index_groups=teams, tiled=True
        )

    k_first = jnp.stack([local_potential * orbitals[1], -local_potential * orbitals[0]])
    section = orbitals + TIME_STEP * k_first

    band = lax.axis_index("band")

    def spread(orbital):
        return lax.psum(
            jnp.stack([jnp.where(band == plan[r], orbital, 0.0) for r in range(rounds)]), "band"
        )

    def collect(both):
        near = jnp.where(first_chip, both[0], both[1])
        far = chip_swap(jnp.where(first_chip, both[1], both[0]))
        pair = jnp.stack([near, far])
        other = core_swap(pair)
        return jnp.concatenate([near, other[0], far, other[1]], axis=1)

    block = jnp.arange(parts)[:, None] + jnp.stack([(share ^ k) * parts for k in range(4)])
    order = block[:, :, None] * height + jnp.arange(height, dtype=jnp.int32)
    along_x = hartley_rows(order.reshape(points), points)
    ways = along_x.reshape(parts, 4, height, points)
    width = points // parts
    along = hartley_rows(jnp.arange(points, dtype=jnp.int32), points)
    source_group = jnp.where(first_chip, plan[0], plan[1])
    groups = jnp.arange(occupancy.shape[0], dtype=jnp.int32)
    filled = jnp.sum(jnp.where(groups == source_group, occupancy, 0))

    weights = [jnp.where(j < filled, 2.0, 0.0).astype(jnp.float32) for j in range(count_own)]
    bands = lax.axis_size("band")
    span = 4 * points
    if parts == 1 and span % 128 == 0 and height % 8 == 0 and count_own == rounds == 2 and bands > 2:
        scaled = -MIXING * jnp.stack(weights)
        gathered = gather(section, plan, bands, span)
        near, far = solve(section, gathered, plan, scaled, along_x, bands, span)
        far = chip_swap(far)
    else:
        mine = jnp.where(first_core, section[:, 0], section[:, 1])
        give = jnp.where(first_core, section[:, 1], section[:, 0])
        half = jnp.concatenate([mine, core_swap(give)], axis=1)
        own = jnp.concatenate([half, chip_swap(half)], axis=1)

        kernel = screened_kernel(points, slot * width, width) * (1.0 / (points * points * points))
        def spectrum(source):
            dens_re = source[0] * own[0] + source[1] * own[1]
            dens_im = source[0] * own[1] - source[1] * own[0]
            field = jnp.stack([dens_re, dens_im]).reshape(2, 4 * height, points, points)
            field = mult("pxyz,zk->pxyk", field, along)
            field = turn(mult("pxyz,yk->pxkz", field, along), 2, 1)
            return mult("pxyz,xk->pkyz", field, along_x) * kernel

        def potential_term(source, weight, moved, side):
            rows = ways[:, 2 * side : 2 * side + 2].reshape(-1, points)
            field = turn(mult("pxyz,kx->pkyz", moved, rows), 1, 2)
            field = mult("pxyz,yk->pxkz", field, along)
            field = mult("pxyz,zk->pxyk", field, along)
            v_re, v_im = field.reshape(2, 2 * height, plane)
            s_re, s_im = source[:, 2 * side * height : 2 * (side + 1) * height]
            scale = -MIXING * weight
            return jnp.stack([scale * (s_re * v_re - s_im * v_im), scale * (s_re * v_im + s_im * v_re)])

        both = [spread(section[:, 0])]
        for j in range(1, count_own):
            both[j - 1], orbital = lax.optimization_barrier((both[j - 1], section[:, j]))
            both.append(spread(orbital))
        near = far = 0.0
        for j in range(count_own):
            if j > 0:
                both[j], near, far = lax.optimization_barrier((both[j], near, far))
            source = collect(both[j])
            moved = spectrum(source)
            far = far + potential_term(source, weights[j], moved, 1)
            if j == count_own - 1:
                far = chip_swap(far)
            near = near + potential_term(source, weights[j], moved, 0)
    total = near + far
    kept = total[:, :height]
    got = core_swap(total[:, height:])
    exchange = jnp.stack(
        [jnp.where(first_core, kept, got), jnp.where(first_core, got, kept)], axis=1
    )

    hamil = local_potential * section + exchange
    k_second = jnp.stack([hamil[1], -hamil[0]])
    delta = 0.5 * TIME_STEP * (k_first + k_second)
    inner = jnp.sum(orbitals * delta, axis=(0, 2, 3))
    squared_modulus = jnp.sum(delta * delta, axis=(0, 2, 3))
    energy = jnp.sum(section * hamil, axis=(0, 2, 3))
    inner, squared_modulus, energy = lax.psum(jnp.stack([inner, squared_modulus, energy]), "grid")
    factor = -2.0 * inner / (squared_modulus + 1e-06)
    fresh = orbitals + factor[None, :, None, None] * delta
    own_filled = jnp.sum(jnp.where(groups == band, occupancy, 0))
    filling = jnp.where(jnp.arange(count_own, dtype=jnp.int32) < own_filled, 2.0, 0.0).astype(
        jnp.float32
    )
    return (fresh, filling * energy / (points * points * points))


def solution(mesh):
    return jax.shard_map(
        per_device,
        mesh=mesh,
        in_specs=(P(None, "band", "grid", None), P("grid", None), P(), P()),
        out_specs=(P(None, "band", "grid", None), P("band")),
        check_vma=False,
    )
```

time: 835 us -> 414 us (0.50)
  waiting for transfers between devices: 485 us -> 82.1 us
  Pallas kernels: 0 us -> 272 us
  matrix products: 120 us -> 0 us
  local copies, waits for them, and re-layouts: 131 us -> 13.4 us
  starting transfers between devices: 23.6 us -> 1.04 us
  between operations: 15.9 us -> 3.43 us
  other arithmetic: 46.2 us -> 34.3 us
    pallas_call x0 -> x2, Pallas kernels: none -> 272 us  [the longest x1 156 us: gather(): pl.pallas_call(functools.partial(gather_kernel, bands), out_shape=(whole,...]
    all_to_all x4 -> x0, waiting for transfers between devices: 250 us -> none  [the longest x2 125 us: screened_solve(): lax.all_to_all(moved, 'grid', split_axis=1, concat_axis=2, tiled=True)]
    psum x1 -> x0, waiting for transfers between devices: 235 us -> none  [spread(): return lax.psum(jnp.where(mine, shard, jnp.zeros_like(shard)), axis)]
    dot_general x12 -> x0, matrix products: 120 us -> none  [mult(): return jnp.einsum(form, left, right, precision=lax.Precision.HIGHEST)]
    ppermute x0 -> x2, waiting for transfers between devices: none -> 82.1 us  [swap(): lax.ppermute(value, 'grid', [(g, (g // parts ^ bit) * parts + g % parts)...]
    transpose x4 -> x0, local copies, waits for them, and re-layouts: 37.2 us -> none  [mult(): return jnp.einsum(form, left, right, precision=lax.Precision.HIGHEST)]
    all_to_all x4 -> x0, local copies, waits for them, and re-layouts: 28.4 us -> none  [the longest x2 18.3 us: screened_solve(): lax.all_to_all(spectrum, 'grid', split_axis=2, concat_axis=1, tiled=True)]
    squeeze x4 -> x0, local copies, waits for them, and re-layouts: 24.6 us -> none  [the longest x2 12.4 us: exchange_terms(): solved[1]]
  transfers between devices with their start and end apart: 5 -> 2, of which waited for: 5 -> 2; matrix products, arithmetic and copies ran while one was open for 20% -> 0% of each run, Pallas kernels for 0% -> 0%
where the time goes in v1:
time: 414 us; the launch traced here: 413 us
  Pallas kernels  272 us (66%)
  waiting for transfers between devices  82.1 us (20%)
  other arithmetic  34.3 us (8%)
  local copies, waits for them, and re-layouts  13.4 us (3%)
  blocking collectives  6.35 us (2%)
    pallas_call x1, Pallas kernels, gather(): pl.pallas_call(functools.partial(gather_kernel, bands), out_shape=(whole,...  156 us
    pallas_call x1, Pallas kernels, solve(): pl.pallas_call(functools.partial(solve_kernel, points), grid_spec=pltpu.P...  116 us
    ppermute x2, waiting for transfers between devices, swap(): lax.ppermute(value, 'grid', [(g, (g // parts ^ bit) * parts + g % parts)...  82.1 us
  transfers between devices with their start and end apart: 2, of which 2 were waited for; matrix products, arithmetic and copies ran while one was open for 0% of the time, Pallas kernels for 0%

profile of v1, /device:TPU:0, one launch (start us, length us, event | category | flops | bytes accessed | tf_op | source)
XLA Modules:
  0.0 412.6 jit_solution(5289298017175505642)
XLA Ops:
  0.7 1.3 fusion.22
  3.3 1.3 fusion.15
  8.6 2.1 neg.20
  10.8 1.4 multiply_bitcast_fusion
  12.2 2.5 reshape.121
  14.8 2.0 fusion.1
  16.8 2.3 reshape.120
  21.9 1.7 slice_multiply_fusion.1
  23.6 1.2 copy-done.1
  25.4 2.3 multiply_add_fusion.1.section.o0
  27.7 156.4 %shard_map.59 = (f32[24,2,2,24,384]{4,3,2,1,0:T(8,128)}, f32[2,2,24,9216]{3,2,1,0:T(8,128)}, f32[24,2,2,24,384]{4,3,2,1,0:T(8,128)}, f32[2,31,2,2,24,384]{5,4,3,2,1,0:T(8,128)}, f32[2,31,2,2,24,384]{5,4,3,2,1,0:T(8,128)}) custom-call(s32[2]{0:T(128)} %plan.1, f32[2,2,24,9216]{3,2,1,0:T(8,128)} %multiply_add_fusion.1.section.o0), custom_call_target="tpu_custom_call" | custom-call | tf_op jit(solution)/shard_map/pallas_call | solution.py:212
  185.6 1.6 pad_maximum_fusion.2.zcut_low
  187.2 1.6 pad_maximum_fusion.1.zcut_high
  189.4 115.7 %shard_map.60 = (f32[2,48,9216]{2,1,0:T(8,128)}, f32[2,48,9216]{2,1,0:T(8,128)}) custom-call(s32[3]{0:T(128)} %pad_add_fusion.info, f32[2]{0:T(128)} %maximum_multiply_fusion.weight, f32[96]{0:T(128)} %copy-done.12, f32[96]{0:T(128)} %copy-done.11, f32[2,31,2,2,24,384]{5,4,3,2,1,0:T(8,128)} %get-tuple-element.9.s0.s2, ...), custom_call_target="tpu_custom_call" | custom-call | tf_op jit(solution)/shard_map/pallas_call | solution.py:434
  306.1 78.0 %collective-permute-done = f32[2,48,9216]{2,1,0:T(8,128)S(1)} collective-permute-done((f32[2,48,9216]{2,1,0:T(8,128)}, f32[2,48,9216]{2,1,0:T(8,128)S(1)}, u32[]{:S(2)}, u32[]{:S(2)}) %collective-permute-start) | collective-permute-done | bytes 3538976 | tf_op jit(solution)/shard_map/ppermute | solution.py:481
  384.2 2.5 add.145
  386.7 1.8 copy-done.7
  388.5 1.4 slice.55
  389.8 4.0 collective-permute-done.1
  393.8 2.4 select_bitcast_fusion.1
  396.3 1.4 multiply_reduce_fusion
  397.9 1.5 multiply_reduce_fusion.2
  399.7 6.4 %psum.7 = f32[3,2]{1,0:T(4,128)S(1)} all-reduce(f32[3,2]{1,0:T(4,128)S(1)} %pad_maximum_fusion.4), channel_id=1, replica_groups=mesh['band'=8,'grid'=4] {'grid'}, use_global_device_ids=true, to_apply=%region_4.5 | all-reduce | flops 6 | bytes 48 | tf_op jit(solution)/shard_map/psum | solution.py:585
  407.2 5.4 %multiply_add_fusion = f32[2,2,24,9216]{3,2,1,0:T(8,128)} fusion(f32[2,2,24,9216]{3,2,1,0:T(8,128)S(1)} %copy-done, f32[2]{0:T(128)S(1)} %multiply_bitcast_fusion.2, f32[1,2,24,9216]{3,2,1,0:T(8,128)} %copy-done.6, f32[1,2,24,9216]{3,2,1,0:T(8,128)} %copy-done.5, f32[1,2,24,9216]{3,2,1,0:T(8,128)} %copy-done.3, f32[1,2,24,9216]{3,2,1,0:T(8,128)} %copy-done.1), kind=kLoop, calls=%fused_computation.3 | loop fusion | flops 4423680 | bytes 14155784 | tf_op jit(solution)/shard_map/add | solution.py:587
  (55 shorter events, 10.8 us)
Async XLA Ops:
  0.7 184.1 %copy-start.11 = (f32[96]{0:T(128)}, f32[96]{0:T(128)S(1)}, u32[]{:S(2)}) copy-start(f32[96]{0:T(128)S(1)} %multiply_exponential_fusion.decay_z) | copy-start | bytes 1156
  0.7 6.5 %copy-start.12 = (f32[96]{0:T(128)}, f32[96]{0:T(128)S(1)}, u32[]{:S(2)}) copy-start(f32[96]{0:T(128)S(1)} %fusion.19.square_z) | copy-start | bytes 1156
  10.8 11.1 %copy-start = (f32[2,2,24,9216]{3,2,1,0:T(8,128)S(1)}, f32[2,2,24,9216]{3,2,1,0:T(8,128)}, u32[]{:S(2)}) copy-start(f32[2,2,24,9216]{3,2,1,0:T(8,128)} %param.4) | copy-start | bytes 10616836
  20.3 0.8 copy-start.9
  20.3 0.9 copy-start.10
  23.6 1.2 copy-start.1
  23.6 1.8 copy-start.3
  27.7 157.1 %copy-start.13 = (f32[96]{0:T(128)S(1)}, f32[96]{0:T(128)}, u32[]{:S(2)}) copy-start(f32[96]{0:T(128)} %copy-done.12) | copy-start | bytes 1156
  305.1 79.1 %collective-permute-start = (f32[2,48,9216]{2,1,0:T(8,128)}, f32[2,48,9216]{2,1,0:T(8,128)S(1)}, u32[]{:S(2)}, u32[]{:S(2)}) collective-permute-start(f32[2,48,9216]{2,1,0:T(8,128)} %get-tuple-element.15), channel_id=1, source_target_pairs={{0,2},{1,3},{2,0},{3,1},{4,6},{5,7},{6,4},{7,5},{8,10},{9,11},{10,... | collective-permute-start | bytes 10616840 | tf_op jit(solution)/shard_map/ppermute | solution.py:481
  386.7 1.8 copy-start.7
  389.8 4.0 collective-permute-start.1
  389.8 6.4 %copy-start.2 = (f32[1,2,24,9216]{3,2,1,0:T(8,128)S(1)}, f32[1,2,24,9216]{3,2,1,0:T(8,128)}, u32[]{:S(2)}) copy-start(f32[1,2,24,9216]{3,2,1,0:T(8,128)} %copy-done.1) | copy-start | bytes 5308420
  389.8 6.4 %copy-start.4 = (f32[1,2,24,9216]{3,2,1,0:T(8,128)S(1)}, f32[1,2,24,9216]{3,2,1,0:T(8,128)}, u32[]{:S(2)}) copy-start(f32[1,2,24,9216]{3,2,1,0:T(8,128)} %copy-done.3) | copy-start | bytes 5308420
  389.8 6.5 %copy-start.8 = (f32[24,9216]{1,0:T(8,128)S(1)}, f32[24,9216]{1,0:T(8,128)}, u32[]{:S(2)}) copy-start(f32[24,9216]{1,0:T(8,128)} %param.5) | copy-start | bytes 2654212
  397.9 1.5 copy-start.5
  397.9 1.8 copy-start.6

commit v2 on v1

--- a/solution.py
+++ b/solution.py
@@ -3,6 +3,8 @@
 
 import jax
 import jax.numpy as jnp
+import ml_dtypes
+import numpy as np
 from jax import lax
 from jax.experimental import pallas as pl
 from jax.experimental.pallas import tpu as pltpu
@@ -107,12 +109,14 @@
             section.at[:, :, :, lanes(k)], cross.at[k], cross_send.at[k], cross_recv.at[k], partner
         )
 
-    def ring_copy(way, t):
+    lines = [(way, part) for part in range(2) for way in range(2)]
+
+    def ring_copy(way, part, t):
         return remote(
-            stream.at[way, t],
-            landed.at[way, t],
-            ring_send.at[way, t],
-            ring_recv.at[way, t],
+            stream.at[way, t, part],
+            landed.at[way, t, part],
+            ring_send.at[way, part, t],
+            ring_recv.at[way, part, t],
             ring[way],
         )
 
@@ -139,36 +143,37 @@
         keep_copy(part + 1).start()
 
     root = plan[lax.div(here, 2)]
-    mine = jnp.full(stream.shape[2:], root, jnp.int32) == band
+    mine = jnp.full(stream.shape[3:], root, jnp.int32) == band
 
     @pl.loop(0, half)
     def _(k):
         cross_copy(k).start()
         cross_copy(half + k).start()
 
-    for way in range(2):
-        stream[way, 0] = section[:, :, :, way * half * width : (way * half + 1) * width]
-        ring_copy(way, 0).start()
+    for way, part in lines:
+        stream[way, 0, part] = section[part, :, :, way * half * width : (way * half + 1) * width]
+        ring_copy(way, part, 0).start()
     side_copy(0).start()
 
     @pl.loop(1, half)
     def _(t):
-        for way in range(2):
-            ring_copy(way, t - 1).wait_recv()
-            own = section[:, :, :, lanes(way * half + t)]
-            stream[way, t] = jnp.where(mine, own, landed[way, t - 1])
-            ring_copy(way, t).start()
+        for way, part in lines:
+            ring_copy(way, part, t - 1).wait_recv()
+            own = section[part, :, :, lanes(way * half + t)]
+            stream[way, t, part] = jnp.where(mine, own, landed[way, t - 1, part])
+            ring_copy(way, part, t).start()
 
     store(0)
 
     @pl.loop(half, chunks)
     def _(t):
         for way in range(2):
-            k = way * half + t - half
-            cross_copy(k).wait_recv()
-            ring_copy(way, t - 1).wait_recv()
-            stream[way, t] = jnp.where(mine, cross[k], landed[way, t - 1])
-            ring_copy(way, t).start()
+            cross_copy(way * half + t - half).wait_recv()
+        for way, part in lines:
+            ring_copy(way, part, t - 1).wait_recv()
+            own = cross[way * half + t - half, part]
+            stream[way, t, part] = jnp.where(mine, own, landed[way, t - 1, part])
+            ring_copy(way, part, t).start()
 
     store(1)
     side_copy(1).start()
@@ -176,14 +181,14 @@
 
     @pl.loop(chunks, steps)
     def _(t):
-        for way in range(2):
-            ring_copy(way, t - 1).wait_recv()
-            stream[way, t] = landed[way, t - 1]
-            ring_copy(way, t).start()
-
-    for way in range(2):
-        ring_copy(way, steps - 1).wait_recv()
-        stream[way, steps] = landed[way, steps - 1]
+        for way, part in lines:
+            ring_copy(way, part, t - 1).wait_recv()
+            stream[way, t, part] = landed[way, t - 1, part]
+            ring_copy(way, part, t).start()
+
+    for way, part in lines:
+        ring_copy(way, part, steps - 1).wait_recv()
+        stream[way, steps, part] = landed[way, steps - 1, part]
     store(2)
 
     @pl.loop(0, chunks)
@@ -192,8 +197,8 @@
 
     @pl.loop(0, steps)
     def _(t):
-        for way in range(2):
-            ring_copy(way, t).wait_send()
+        for way, part in lines:
+            ring_copy(way, part, t).wait_send()
 
     for k in range(5):
         side_copy(k).wait()
@@ -223,8 +228,8 @@
             pltpu.VMEM(log.shape, jnp.float32),
             dma((chunks,)),
             dma((chunks,)),
-            dma((2, steps)),
-            dma((2, steps)),
+            dma((2, 2, steps)),
+            dma((2, 2, steps)),
             dma((5,)),
             dma((5,)),
             dma((4,)),
@@ -250,10 +255,13 @@
     return dot(left[0], right[0], axis) + (dot(left[0], right[1], axis) + dot(left[1], right[0], axis))
 
 
-def solve_kernel(
+def concat(pieces):
+    return jnp.concatenate(pieces, axis=0)
+
+
+def forward_kernel(
     points,
     info,
-    weight,
     square_z,
     decay_z,
     s0,
@@ -266,51 +274,45 @@
     o3,
     zcut_high,
     zcut_low,
-    z_high,
-    z_low,
     x_high,
     x_low,
     y_pair,
     y_low,
     square_xy,
     decay_xy,
-    near,
-    far,
     work,
 ):
-    phase, step = pl.program_id(0), pl.program_id(1)
-    width = near.shape[-1]
+    step = pl.program_id(0)
+    width = x_high.shape[0]
     tiles = work.shape[0]
     window = zcut_high.shape[2]
     rows = pl.ds(pl.multiple_of(step * width, width), width)
 
     def source(part, j):
-        return jnp.concatenate([s[0, 0, part, j] for s in (s0, s1, s2, s3)], axis=0)
-
-    @pl.when(phase == 0)
-    def _():
-        own_re, own_im = (
-            jnp.concatenate([o0[p, 0], o1[p, 0], o2[0, p, 0], o3[0, p, 0]], axis=0)
-            for p in range(2)
-        )
-        fields = []
-        for j in range(2):
-            s_re, s_im = source(0, j), source(1, j)
-            fields.append(s_re * own_re + s_im * own_im)
-            fields.append(s_re * own_im - s_im * own_re)
-        high, low = halves(jnp.concatenate(fields, axis=0))
-        parts = []
-        for k in range(2):
-            cut = slice(k * (width - window), k * (width - window) + window)
-            parts.append(
-                three((zcut_high[k], zcut_low[k]), (high[:, cut], low[:, cut]), 1)
-            )
-        along = halves(jnp.concatenate(parts, axis=0))
-        out = three(along, (x_high[...], x_low[...]))
-        for k in range(tiles):
-            work[k, rows, :] = out[:, 128 * k : 128 * (k + 1)]
-
-    @pl.when(jnp.logical_and(phase == 0, step == pl.num_programs(1) - 1))
+        return concat([s[0, 0, part, j] for s in (s0, s1, s2, s3)])
+
+    own_re, own_im = (
+        jnp.concatenate([o0[p, 0], o1[p, 0], o2[0, p, 0], o3[0, p, 0]], axis=0)
+        for p in range(2)
+    )
+    fields = []
+    for j in range(2):
+        s_re, s_im = source(0, j), source(1, j)
+        fields.append(s_re * own_re + s_im * own_im)
+        fields.append(s_re * own_im - s_im * own_re)
+    high, low = halves(jnp.concatenate(fields, axis=0))
+    parts = []
+    for k in range(2):
+        cut = slice(k * (width - window), k * (width - window) + window)
+        parts.append(
+            three((zcut_high[k], zcut_low[k]), (high[:, cut], low[:, cut]), 1)
+        )
+    along = halves(jnp.concatenate(parts, axis=0))
+    out = three(along, (x_high[...], x_low[...]))
+    for k in range(tiles):
+        work[k, rows, :] = out[:, 128 * k : 128 * (k + 1)]
+
+    @pl.when(step == pl.num_programs(0) - 1)
     def _():
         scale = 1.0 / (points * points * points)
 
@@ -340,30 +342,40 @@
                         at = 128 * (u * tiles + k)
                         work[k, lines[u], :] = value[:, at : at + 128]
 
-    @pl.when(phase == 1)
-    def _():
-        spectrum = halves(jnp.concatenate([work[k, rows, :] for k in range(tiles)], axis=1))
-        along = halves(three((x_high[...], x_low[...]), spectrum, 1))
-        field = three(along, (z_high[...], z_low[...]))
-        term_re = term_im = 0.0
-        for j in range(2):
-            v_re = field[2 * j * points : (2 * j + 1) * points]
-            v_im = field[(2 * j + 1) * points : (2 * j + 2) * points]
-            s_re, s_im = source(0, j), source(1, j)
-            term_re = term_re + weight[j] * (s_re * v_re - s_im * v_im)
-            term_im = term_im + weight[j] * (s_re * v_im + s_im * v_re)
-        middle = points // 2
-        for k, term in enumerate((term_re, term_im)):
-            near[k] = term[:middle]
-            far[k] = term[middle:]
-
-
-def solve(section, gathered, plan, weights, along_x, bands, width):
+def inverse_kernel(info, weight, work, s0, s1, x_high, x_low, z_high, z_low, term):
+    middle = term.shape[1]
+    spectrum = halves(jnp.concatenate([work[k] for k in range(work.shape[0])], axis=1))
+    along = halves(three((x_high[...], x_low[...]), spectrum, 1))
+    field = three(along, (z_high[...], z_low[...]))
+    term_re = term_im = 0.0
+    for j in range(2):
+        v_re = field[2 * j * middle : (2 * j + 1) * middle]
+        v_im = field[(2 * j + 1) * middle : (2 * j + 2) * middle]
+        s_re, s_im = (concat([s[0, 0, part, j] for s in (s0, s1)]) for part in range(2))
+        term_re = term_re + weight[j] * (s_re * v_re - s_im * v_im)
+        term_im = term_im + weight[j] * (s_re * v_im + s_im * v_re)
+    term[0] = term_re
+    term[1] = term_im
+
+
+def numpy_hartley(points):
+    index = np.arange(points)
+    angle = index[:, None] * index[None, :] % points * (2.0 * math.pi / points)
+    return np.cos(angle) + np.sin(angle)
+
+
+def numpy_split(value):
+    high = value.astype(ml_dtypes.bfloat16)
+    return high, (value - high.astype(np.float64)).astype(ml_dtypes.bfloat16)
+
+
+def solve(section, gathered, plan, weights, bands, width):
     cross, side, side_cross, stream, side_stream = gathered
     height, plane = section.shape[2], section.shape[3]
-    points = along_x.shape[0]
+    points = 4 * height
     chunks = plane // width
     half = chunks // 2
+    middle = points // 2
     here = lax.axis_index("grid")
     place = ring_place(lax.axis_index("band"), bands)
     root = ring_place(jnp.where(here // 2 == 0, plan[0], plan[1]), bands)
@@ -371,87 +383,84 @@
         [lax.rem(place - root + bands, bands), lax.rem(root - place + bands, bands), here % 2]
     ).astype(jnp.int32)
 
-    index = jnp.arange(points, dtype=jnp.int32)
-    along = hartley_rows(index, points)
-    four = jnp.eye(4, dtype=jnp.float32)
-
-    def blocks(matrix):
-        return jnp.einsum("ab,ij->aibj", four, matrix).reshape(width, width)
-
-    def split(value):
-        high = lax.reduce_precision(value, 8, 7)
-        return high.astype(jnp.bfloat16), (value - high).astype(jnp.bfloat16)
-
-    z_high, z_low = split(blocks(along))
-    x_high, x_low = split(blocks(along_x))
-    y_high, y_low = split(along)
+    along = numpy_hartley(points)
+    orders = [
+        np.concatenate([(g ^ k) * height + np.arange(height) for k in range(4)]) for g in range(4)
+    ]
+    x_all = np.stack([np.kron(np.eye(4), along[order]) for order in orders])
+    x_sides = x_all.reshape(4, 4, 2, middle, width)
+
+    def pick(table):
+        return [
+            lax.dynamic_index_in_dim(jnp.asarray(piece), here, 0, keepdims=False)
+            for piece in numpy_split(table)
+        ]
+
+    x_high, x_low = pick(x_all)
+    z_high, z_low = numpy_split(np.kron(np.eye(4), along))
+    y_high, y_low = numpy_split(along)
     window = -(-(width // 2) // 128) * 128
 
     def cuts(matrix):
-        return jnp.stack([matrix[: width // 2, :window], matrix[width // 2 :, width - window :]])
-
-    fold = jnp.where(index <= points // 2, index, index - points).astype(jnp.float32)
-    base = 2.0 * math.pi / BOX
-    square = base * base * (fold * fold)
-    decay = jnp.exp(-square / (4.0 * OMEGA * OMEGA))
-    square_x, decay_x = jnp.tile(square, 4), jnp.tile(decay, 4)
-    square_xy = square[:, None] + square_x[None, :]
-    decay_xy = decay[:, None] * decay_x[None, :]
+        return jnp.asarray(
+            np.stack([matrix[: width // 2, :window], matrix[width // 2 :, width - window :]])
+        )
+
+    index = np.arange(points)
+    fold = np.where(index <= points // 2, index, index - points)
+    square = (2.0 * math.pi / BOX) ** 2 * (fold * fold)
+    decay = np.exp(-square / (4.0 * OMEGA * OMEGA))
+
+    def single(value):
+        return jnp.asarray(value.astype(np.float32))
+
     tables = [
         cuts(z_high),
         cuts(z_low),
-        z_high,
-        z_low,
         x_high,
         x_low,
-        jnp.concatenate([y_high, y_high], axis=1),
-        y_low,
-        square_xy,
-        decay_xy,
+        jnp.asarray(np.concatenate([y_high, y_high], axis=1)),
+        jnp.asarray(y_low),
+        single(square[:, None] + np.tile(square, 4)[None, :]),
+        single(decay[:, None] * np.tile(decay, 4)[None, :]),
     ]
 
     def line(offset):
-        def spot(p, i, info):
+        def spot(i, info):
             way = lax.div(i, half)
             return (way, info[way] + lax.rem(i, half) + offset, 0, 0, 0, 0)
 
         return pl.BlockSpec((1, 1, 2, 2, height, width), spot)
 
-    natural = pl.BlockSpec(
-        (2, 1, height, width), lambda p, i, info: (0, info[2], 0, (1 - p) * i + p * (chunks - 1))
-    )
-    piece = pl.BlockSpec(
-        (1, 2, 1, height, width),
-        lambda p, i, info: ((1 - p) * i + p * (chunks - 1), 0, info[2], 0, 0),
-    )
+    natural = pl.BlockSpec((2, 1, height, width), lambda i, info: (0, info[2], 0, i))
+    piece = pl.BlockSpec((1, 2, 1, height, width), lambda i, info: (i, 0, info[2], 0, 0))
     scalars = pl.BlockSpec(memory_space=pltpu.SMEM)
-    result = pl.BlockSpec((2, 2 * height, width), lambda p, i, info: (0, 0, p * i))
+    tiles = width // 128
 
     def full(table):
-        return pl.BlockSpec(table.shape, lambda p, i, info: (0,) * table.ndim)
-
-    half_grid = jax.ShapeDtypeStruct((2, 2 * height, plane), jnp.float32)
-    return pl.pallas_call(
-        functools.partial(solve_kernel, points),
+        return pl.BlockSpec(table.shape, lambda i, info: (0,) * table.ndim)
+
+    spectrum = jax.ShapeDtypeStruct((tiles, plane, 128), jnp.float32)
+    params = pltpu.CompilerParams(
+        dimension_semantics=("arbitrary",), vmem_limit_bytes=VMEM_BYTES
+    )
+    work = pl.pallas_call(
+        functools.partial(forward_kernel, points),
         grid_spec=pltpu.PrefetchScalarGridSpec(
             num_scalar_prefetch=1,
-            grid=(2, chunks),
-            in_specs=[scalars] * 3
+            grid=(chunks,),
+            in_specs=[scalars] * 2
             + [line(0), line(0), line(half), line(half)]
             + [natural, natural, piece, piece]
             + [full(table) for table in tables],
-            out_specs=[result, result],
-            scratch_shapes=[pltpu.VMEM((width // 128, plane, 128), jnp.float32)],
+            out_specs=full(spectrum),
         ),
-        out_shape=(half_grid, half_grid),
-        compiler_params=pltpu.CompilerParams(
-            dimension_semantics=("arbitrary", "arbitrary"), vmem_limit_bytes=VMEM_BYTES
-        ),
+        out_shape=spectrum,
+        compiler_params=params,
     )(
         info,
-        weights,
-        square,
-        decay,
+        single(square),
+        single(decay),
         stream,
         side_stream,
         stream,
@@ -462,6 +471,31 @@
         side_cross,
         *tables,
     )
+
+    def inverse(part):
+        constants = [
+            *pick(x_sides[:, :, part].reshape(4, 4 * middle, width)),
+            jnp.asarray(z_high),
+            jnp.asarray(z_low),
+        ]
+        return pl.pallas_call(
+            inverse_kernel,
+            grid_spec=pltpu.PrefetchScalarGridSpec(
+                num_scalar_prefetch=1,
+                grid=(chunks,),
+                in_specs=[scalars, pl.BlockSpec((tiles, width, 128), lambda i, info: (0, i, 0))]
+                + [line(part * half)] * 2
+                + [full(table) for table in constants],
+                out_specs=pl.BlockSpec((2, middle, width), lambda i, info: (0, 0, i)),
+            ),
+            out_shape=jax.ShapeDtypeStruct((2, middle, plane), jnp.float32),
+            compiler_params=params,
+            cost_estimate=pl.CostEstimate(
+                flops=24 * middle * width * plane, bytes_accessed=32 * plane * width, transcendentals=0
+            ),
+        )(info, weights, work, stream, side_stream, *constants)
+
+    return inverse
 
 
 def per_device(orbitals, local_potential, plan, occupancy):
@@ -528,8 +562,9 @@
     if parts == 1 and span % 128 == 0 and height % 8 == 0 and count_own == rounds == 2 and bands > 2:
         scaled = -MIXING * jnp.stack(weights)
         gathered = gather(section, plan, bands, span)
-        near, far = solve(section, gathered, plan, scaled, along_x, bands, span)
-        far = chip_swap(far)
+        inverse = solve(section, gathered, plan, scaled, bands, span)
+        far = chip_swap(inverse(1))
+        near = inverse(0)
     else:
         mine = jnp.where(first_core, section[:, 0], section[:, 1])
         give = jnp.where(first_core, section[:, 1], section[:, 0])
@@ -569,9 +604,8 @@
             if j == count_own - 1:
                 far = chip_swap(far)
             near = near + potential_term(source, weights[j], moved, 0)
-    total = near + far
-    kept = total[:, :height]
-    got = core_swap(total[:, height:])
+    got = core_swap(near[:, height:] + far[:, height:])
+    kept = near[:, :height] + far[:, :height]
     exchange = jnp.stack(
         [jnp.where(first_core, kept, got), jnp.where(first_core, got, kept)], axis=1
     )

time: 414 us -> 361 us (0.87)
  waiting for transfers between devices: 82.1 us -> 50.9 us
  other arithmetic: 34.3 us -> 20.3 us
  Pallas kernels: 272 us -> 262 us
    ppermute x2, waiting for transfers between devices: 82.1 us -> 50.9 us  [swap(): lax.ppermute(value, 'grid', [(g, (g // parts ^ bit) * parts + g % parts)...]
    pallas_call x1, Pallas kernels: 156 us -> 129 us  [gather(): pl.pallas_call(functools.partial(gather_kernel, bands), out_shape=(whole,...]
    pallas_call x1 -> x3, Pallas kernels: 116 us -> 133 us  [the longest x1 75.4 us: solve(): pl.pallas_call(functools.partial(forward_kernel, points), grid_spec=pltpu...]
    squeeze x0 -> x3, local copies, waits for them, and re-layouts: none -> 5.4 us  [pick(): lax.dynamic_index_in_dim(jnp.asarray(piece), here, 0, keepdims=False)]
    reshape x2 -> x0, local copies, waits for them, and re-layouts: 4.89 us -> none  [blocks(): return jnp.einsum('ab,ij->aibj', four, matrix).reshape(width, width)]
    convert_element_type x4 -> x0, other arithmetic: 4.19 us -> none  [split(): return (high.astype(jnp.bfloat16), (value - high).astype(jnp.bfloat16))]
  transfers between devices with their start and end apart: 2 -> 2, of which waited for: 2 -> 2; matrix products, arithmetic and copies ran while one was open for 0% -> 0% of each run, Pallas kernels for 0% -> 8%
where the time goes in v2:
time: 361 us; the launch traced here: 359 us
  Pallas kernels  262 us (73%)
  waiting for transfers between devices  50.9 us (14%)
  other arithmetic  20.3 us (6%)
  local copies, waits for them, and re-layouts  14.4 us (4%)
  blocking collectives  6.74 us (2%)
    pallas_call x1, Pallas kernels, gather(): pl.pallas_call(functools.partial(gather_kernel, bands), out_shape=(whole,...  129 us
    pallas_call x1, Pallas kernels, solve(): pl.pallas_call(functools.partial(forward_kernel, points), grid_spec=pltpu...  75.4 us
    pallas_call x2, Pallas kernels, inverse(): pl.pallas_call(inverse_kernel, grid_spec=pltpu.PrefetchScalarGridSpec(num...  58.1 us
    ppermute x2, waiting for transfers between devices, swap(): lax.ppermute(value, 'grid', [(g, (g // parts ^ bit) * parts + g % parts)...  50.9 us
  transfers between devices with their start and end apart: 2, of which 2 were waited for; matrix products, arithmetic and copies ran while one was open for 0% of the time, Pallas kernels for 8%

profile of v2, /device:TPU:0, one launch (start us, length us, event | category | flops | bytes accessed | tf_op | source)
XLA Modules:
  0.0 359.1 jit_solution(14699604282315927524)
XLA Ops:
  0.6 1.3 fusion.5
  3.3 1.4 fusion.1
  6.0 1.2 neg.7
  7.2 2.8 slice_multiply_fusion.1
  11.8 2.1 copy.25.section.o0
  13.9 128.5 %shard_map.203 = (f32[24,2,2,24,384]{4,3,2,1,0:T(8,128)}, f32[2,2,24,9216]{3,2,1,0:T(8,128)}, f32[24,2,2,24,384]{4,3,2,1,0:T(8,128)}, f32[2,31,2,2,24,384]{5,4,3,2,1,0:T(8,128)}, f32[2,31,2,2,24,384]{5,4,3,2,1,0:T(8,128)}) custom-call(s32[2]{0:T(128)} %plan.1, f32[2,2,24,9216]{3,2,1,0:T(8,128)} %copy.25.section.o0), custom_call_target="tpu_custom_call" | custom-call | tf_op jit(solution)/shard_map/pallas_call | solution.py:217
  143.0 1.9 dynamic-slice_bitcast_fusion
  144.9 1.7 dynamic-slice_bitcast_fusion.2
  147.3 75.4 %shard_map.204.work = f32[3,9216,128]{2,1,0:T(8,128)} custom-call(s32[3]{0:T(128)} %pad_add_fusion.info, f32[96]{0:T(128)} %constant.144.clone.square_z, f32[96]{0:T(128)} %constant.145.clone.decay_z, f32[2,31,2,2,24,384]{5,4,3,2,1,0:T(8,128)} %get-tuple-element.7.s0.s2, f32[2,31,2,2,24,384]{5,4,3,2,1,0:T(8,128)} %get-tuple-element.8.s1.s3, ...), custom_call_target="tpu_custom_call" | custom-call | tf_op jit(solution)/shard_map/pallas_call | solution.py:447
  222.7 29.0 %shard_map.206 = f32[2,48,9216]{2,1,0:T(8,128)} custom-call(s32[3]{0:T(128)} %pad_add_fusion.info, f32[2]{0:T(128)} %maximum_multiply_fusion.weight, f32[3,9216,128]{2,1,0:T(8,128)} %shard_map.204.work, f32[2,31,2,2,24,384]{5,4,3,2,1,0:T(8,128)} %get-tuple-element.7.s0.s2, f32[2,31,2,2,24,384]{5,4,3,2,1,0:T(8,128)} %get-tuple-element.8.s1.s3, ...), custom_call_target="tpu_custom_call" | custom-call | flops 4076863488 | bytes 113246208 | tf_op jit(solution)/shard_map/pallas_call | solution.py:481
  251.7 1.4 collective-permute-start
  253.1 1.7 dynamic-slice_bitcast_fusion.4
  254.8 29.0 %shard_map.205 = f32[2,48,9216]{2,1,0:T(8,128)} custom-call(s32[3]{0:T(128)} %pad_add_fusion.info, f32[2]{0:T(128)} %maximum_multiply_fusion.weight, f32[3,9216,128]{2,1,0:T(8,128)} %shard_map.204.work, f32[2,31,2,2,24,384]{5,4,3,2,1,0:T(8,128)} %get-tuple-element.7.s0.s2, f32[2,31,2,2,24,384]{5,4,3,2,1,0:T(8,128)} %get-tuple-element.8.s1.s3, ...), custom_call_target="tpu_custom_call" | custom-call | flops 4076863488 | bytes 113246208 | tf_op jit(solution)/shard_map/pallas_call | solution.py:481
  283.8 46.9 %collective-permute-done = f32[2,48,9216]{2,1,0:T(8,128)S(1)} collective-permute-done((f32[2,48,9216]{2,1,0:T(8,128)}, f32[2,48,9216]{2,1,0:T(8,128)S(1)}, u32[]{:S(2)}, u32[]{:S(2)}) %collective-permute-start) | collective-permute-done | bytes 3538976 | tf_op jit(solution)/shard_map/ppermute | solution.py:515
  330.7 1.8 copy-done.8
  332.5 2.8 slice_add_fusion
  335.4 4.0 %collective-permute-done.1 = f32[2,24,9216]{2,1,0:T(8,128)} collective-permute-done((f32[2,24,9216]{2,1,0:T(8,128)}, f32[2,24,9216]{2,1,0:T(8,128)}, u32[]{:S(2)}, u32[]{:S(2)}) %collective-permute-start.1) | collective-permute-done | bytes 1769504 | tf_op jit(solution)/shard_map/ppermute | solution.py:515
  339.4 2.9 select_bitcast_fusion.1
  342.3 1.1 multiply_reduce_fusion
  343.7 1.2 multiply_reduce_fusion.2
  345.5 6.7 %psum.7 = f32[3,2]{1,0:T(4,128)S(1)} all-reduce(f32[3,2]{1,0:T(4,128)S(1)} %pad_maximum_fusion.1), channel_id=1, replica_groups=mesh['band'=8,'grid'=4] {'grid'}, use_global_device_ids=true, to_apply=%region_4.5 | all-reduce | flops 6 | bytes 48 | tf_op jit(solution)/shard_map/psum | solution.py:619
  352.2 3.7 %multiply_add_fusion = f32[2,2,24,9216]{3,2,0,1:T(8,128)S(1)} fusion(f32[2]{0:T(128)S(1)} %multiply_bitcast_fusion, f32[2,2,24,9216]{3,2,1,0:T(8,128)S(1)} %copy-done, f32[1,2,24,9216]{3,2,0,1:T(8,128)} %copy-done.6, f32[1,2,24,9216]{3,2,0,1:T(8,128)} %copy-done.5, f32[1,2,24,9216]{3,2,0,1:T(8,128)} %copy-done.3, f32[1,2,24,9216]{3,2,0,1:T(8,128)} %copy-done.1), kind=kLoop, calls=%fused_computation.3 | loop fusion | flops 4423680 | bytes 14155784 | tf_op jit(solution)/shard_map/add | solution.py:621
  355.9 2.0 copy.29
  357.9 1.2 fusion.3
  (24 shorter events, 3.9 us)
Async XLA Ops:
  7.2 3.3 copy-start
  10.0 1.2 copy-start.1
  10.0 1.8 copy-start.3
  251.7 79.0 %collective-permute-start = (f32[2,48,9216]{2,1,0:T(8,128)}, f32[2,48,9216]{2,1,0:T(8,128)S(1)}, u32[]{:S(2)}, u32[]{:S(2)}) collective-permute-start(f32[2,48,9216]{2,1,0:T(8,128)} %shard_map.206), channel_id=1, source_target_pairs={{0,2},{1,3},{2,0},{3,1},{4,6},{5,7},{6,4},{7,5},{8,10},{9,11},{10,... | collective-permute-start | bytes 10616840 | tf_op jit(solution)/shard_map/ppermute | solution.py:515
  330.7 1.8 copy-start.8
  335.4 4.0 %collective-permute-start.1 = (f32[2,24,9216]{2,1,0:T(8,128)}, f32[2,24,9216]{2,1,0:T(8,128)}, u32[]{:S(2)}, u32[]{:S(2)}) collective-permute-start(f32[2,24,9216]{2,1,0:T(8,128)} %slice_add_fusion), channel_id=1, source_target_pairs={{0,1},{1,0},{2,3},{3,2},{4,5},{5,4},{6,7},{7,6},{8,9},{9,8},{10,11... | collective-permute-start | bytes 5308424 | tf_op jit(solution)/shard_map/ppermute | solution.py:515
  335.4 6.9 %copy-start.2 = (f32[1,2,24,9216]{3,2,0,1:T(8,128)S(1)}, f32[1,2,24,9216]{3,2,0,1:T(8,128)}, u32[]{:S(2)}) copy-start(f32[1,2,24,9216]{3,2,0,1:T(8,128)} %copy-done.1) | copy-start | bytes 5308420
  335.4 6.9 %copy-start.4 = (f32[1,2,24,9216]{3,2,0,1:T(8,128)S(1)}, f32[1,2,24,9216]{3,2,0,1:T(8,128)}, u32[]{:S(2)}) copy-start(f32[1,2,24,9216]{3,2,0,1:T(8,128)} %copy-done.3) | copy-start | bytes 5308420
  335.4 6.9 %copy-start.7 = (f32[24,9216]{1,0:T(8,128)S(1)}, f32[24,9216]{1,0:T(8,128)}, u32[]{:S(2)}) copy-start(f32[24,9216]{1,0:T(8,128)} %param.21) | copy-start | bytes 2654212
  343.7 1.2 copy-start.5
  343.7 1.8 copy-start.6

commit v3 on v2

--- a/solution.py
+++ b/solution.py
@@ -109,14 +109,14 @@
             section.at[:, :, :, lanes(k)], cross.at[k], cross_send.at[k], cross_recv.at[k], partner
         )
 
-    lines = [(way, part) for part in range(2) for way in range(2)]
+    lines = [(way, (part, j)) for part in range(2) for j in range(2) for way in range(2)]
 
     def ring_copy(way, part, t):
         return remote(
-            stream.at[way, t, part],
-            landed.at[way, t, part],
-            ring_send.at[way, part, t],
-            ring_recv.at[way, part, t],
+            stream.at[way, t, *part],
+            landed.at[way, t, *part],
+            ring_send.at[way, *part, t],
+            ring_recv.at[way, *part, t],
             ring[way],
         )
 
@@ -143,7 +143,7 @@
         keep_copy(part + 1).start()
 
     root = plan[lax.div(here, 2)]
-    mine = jnp.full(stream.shape[3:], root, jnp.int32) == band
+    mine = jnp.full(stream.shape[4:], root, jnp.int32) == band
 
     @pl.loop(0, half)
     def _(k):
@@ -151,7 +151,7 @@
         cross_copy(half + k).start()
 
     for way, part in lines:
-        stream[way, 0, part] = section[part, :, :, way * half * width : (way * half + 1) * width]
+        stream[way, 0, *part] = section[*part, :, way * half * width : (way * half + 1) * width]
         ring_copy(way, part, 0).start()
     side_copy(0).start()
 
@@ -159,8 +159,8 @@
     def _(t):
         for way, part in lines:
             ring_copy(way, part, t - 1).wait_recv()
-            own = section[part, :, :, lanes(way * half + t)]
-            stream[way, t, part] = jnp.where(mine, own, landed[way, t - 1, part])
+            own = section[*part, :, lanes(way * half + t)]
+            stream[way, t, *part] = jnp.where(mine, own, landed[way, t - 1, *part])
             ring_copy(way, part, t).start()
 
     store(0)
@@ -171,8 +171,8 @@
             cross_copy(way * half + t - half).wait_recv()
         for way, part in lines:
             ring_copy(way, part, t - 1).wait_recv()
-            own = cross[way * half + t - half, part]
-            stream[way, t, part] = jnp.where(mine, own, landed[way, t - 1, part])
+            own = cross[way * half + t - half, *part]
+            stream[way, t, *part] = jnp.where(mine, own, landed[way, t - 1, *part])
             ring_copy(way, part, t).start()
 
     store(1)
@@ -183,12 +183,12 @@
     def _(t):
         for way, part in lines:
             ring_copy(way, part, t - 1).wait_recv()
-            stream[way, t, part] = landed[way, t - 1, part]
+            stream[way, t, *part] = landed[way, t - 1, *part]
             ring_copy(way, part, t).start()
 
     for way, part in lines:
         ring_copy(way, part, steps - 1).wait_recv()
-        stream[way, steps, part] = landed[way, steps - 1, part]
+        stream[way, steps, *part] = landed[way, steps - 1, *part]
     store(2)
 
     @pl.loop(0, chunks)
@@ -228,8 +228,8 @@
             pltpu.VMEM(log.shape, jnp.float32),
             dma((chunks,)),
             dma((chunks,)),
-            dma((2, 2, steps)),
-            dma((2, 2, steps)),
+            dma((2, 2, 2, steps)),
+            dma((2, 2, 2, steps)),
             dma((5,)),
             dma((5,)),
             dma((4,)),
@@ -425,9 +425,9 @@
         single(decay[:, None] * np.tile(decay, 4)[None, :]),
     ]
 
-    def line(offset):
+    def line(offset, first=0):
         def spot(i, info):
-            way = lax.div(i, half)
+            way = lax.div(first + i, half)
             return (way, info[way] + lax.rem(i, half) + offset, 0, 0, 0, 0)
 
         return pl.BlockSpec((1, 1, 2, 2, height, width), spot)
@@ -472,7 +472,8 @@
         *tables,
     )
 
-    def inverse(part):
+    def inverse(part, side):
+        first = side * half
         constants = [
             *pick(x_sides[:, :, part].reshape(4, 4 * middle, width)),
             jnp.asarray(z_high),
@@ -482,16 +483,19 @@
             inverse_kernel,
             grid_spec=pltpu.PrefetchScalarGridSpec(
                 num_scalar_prefetch=1,
-                grid=(chunks,),
-                in_specs=[scalars, pl.BlockSpec((tiles, width, 128), lambda i, info: (0, i, 0))]
-                + [line(part * half)] * 2
+                grid=(half,),
+                in_specs=[
+                    scalars,
+                    pl.BlockSpec((tiles, width, 128), lambda i, info: (0, first + i, 0)),
+                ]
+                + [line(part * half, first)] * 2
                 + [full(table) for table in constants],
                 out_specs=pl.BlockSpec((2, middle, width), lambda i, info: (0, 0, i)),
             ),
-            out_shape=jax.ShapeDtypeStruct((2, middle, plane), jnp.float32),
+            out_shape=jax.ShapeDtypeStruct((2, middle, half * width), jnp.float32),
             compiler_params=params,
             cost_estimate=pl.CostEstimate(
-                flops=24 * middle * width * plane, bytes_accessed=32 * plane * width, transcendentals=0
+                flops=12 * middle * width * plane, bytes_accessed=16 * plane * width, transcendentals=0
             ),
         )(info, weights, work, stream, side_stream, *constants)
 
@@ -563,8 +567,8 @@
         scaled = -MIXING * jnp.stack(weights)
         gathered = gather(section, plan, bands, span)
         inverse = solve(section, gathered, plan, scaled, bands, span)
-        far = chip_swap(inverse(1))
-        near = inverse(0)
+        far = [chip_swap(inverse(1, side)) for side in range(2)]
+        near = [inverse(0, side) for side in range(2)]
     else:
         mine = jnp.where(first_core, section[:, 0], section[:, 1])
         give = jnp.where(first_core, section[:, 1], section[:, 0])
@@ -604,8 +608,10 @@
             if j == count_own - 1:
                 far = chip_swap(far)
             near = near + potential_term(source, weights[j], moved, 0)
-    got = core_swap(near[:, height:] + far[:, height:])
-    kept = near[:, :height] + far[:, :height]
+        near, far = [near], [far]
+    got = [core_swap(a[:, height:] + b[:, height:]) for a, b in zip(near, far)]
+    kept = [a[:, :height] + b[:, :height] for a, b in zip(near, far)]
+    got, kept = jnp.concatenate(got, axis=2), jnp.concatenate(kept, axis=2)
     exchange = jnp.stack(
         [jnp.where(first_core, kept, got), jnp.where(first_core, got, kept)], axis=1
     )

time: 361 us -> 332 us (0.920)
  waiting for transfers between devices: 50.9 us -> 27.4 us
  Pallas kernels: 262 us -> 257 us
    ppermute x2 -> x4, waiting for transfers between devices: 50.9 us -> 27.4 us  [swap(): lax.ppermute(value, 'grid', [(g, (g // parts ^ bit) * parts + g % parts)...]
    pallas_call x1, Pallas kernels: 129 us -> 118 us  [gather(): pl.pallas_call(functools.partial(gather_kernel, bands), out_shape=(whole,...]
    pallas_call x2 -> x4, Pallas kernels: 58.1 us -> 63.5 us  [inverse(): pl.pallas_call(inverse_kernel, grid_spec=pltpu.PrefetchScalarGridSpec(num...]
    concatenate x0 -> x2, other arithmetic: none -> 4.44 us  [per_device(): got, kept = (jnp.concatenate(got, axis=2), jnp.concatenate(kept, axis=2))]
  transfers between devices with their start and end apart: 2 -> 4, of which waited for: 2 -> 2; matrix products, arithmetic and copies ran while one was open for 0% -> 2% of each run, Pallas kernels for 8% -> 14%
where the time goes in v3:
time: 332 us; the launch traced here: 331 us
  Pallas kernels  257 us (77%)
  waiting for transfers between devices  27.4 us (8%)
  other arithmetic  21.4 us (6%)
  local copies, waits for them, and re-layouts  13.5 us (4%)
  blocking collectives  5.93 us (2%)
  between operations  3.44 us (1%)
    pallas_call x1, Pallas kernels, gather(): pl.pallas_call(functools.partial(gather_kernel, bands), out_shape=(whole,...  118 us
    pallas_call x1, Pallas kernels, solve(): pl.pallas_call(functools.partial(forward_kernel, points), grid_spec=pltpu...  75.3 us
    pallas_call x4, Pallas kernels, inverse(): pl.pallas_call(inverse_kernel, grid_spec=pltpu.PrefetchScalarGridSpec(num...  63.5 us
    ppermute x4, waiting for transfers between devices, swap(): lax.ppermute(value, 'grid', [(g, (g // parts ^ bit) * parts + g % parts)...  27.4 us
  transfers between devices with their start and end apart: 4, of which 2 were waited for; matrix products, arithmetic and copies ran while one was open for 2% of the time, Pallas kernels for 14%

profile of v3, /device:TPU:0, one launch (start us, length us, event | category | flops | bytes accessed | tf_op | source)
XLA Modules:
  0.0 330.7 jit_solution(3351368592147519433)
XLA Ops:
  0.6 1.3 fusion.9
  3.3 1.4 fusion.5
  6.0 1.2 neg.7
  7.2 2.8 slice_multiply_fusion.1
  11.8 2.1 copy.29.section.o0
  13.9 118.1 %shard_map.239 = (f32[24,2,2,24,384]{4,3,2,1,0:T(8,128)}, f32[2,2,24,9216]{3,2,1,0:T(8,128)}, f32[24,2,2,24,384]{4,3,2,1,0:T(8,128)}, f32[2,31,2,2,24,384]{5,4,3,2,1,0:T(8,128)}, f32[2,31,2,2,24,384]{5,4,3,2,1,0:T(8,128)}) custom-call(s32[2]{0:T(128)} %plan.1, f32[2,2,24,9216]{3,2,1,0:T(8,128)} %copy.29.section.o0), custom_call_target="tpu_custom_call" | custom-call | tf_op jit(solution)/shard_map/pallas_call | solution.py:217
  132.6 1.9 dynamic-slice_bitcast_fusion
  134.6 1.7 dynamic-slice_bitcast_fusion.2
  136.9 75.3 %shard_map.240.work = f32[3,9216,128]{2,1,0:T(8,128)} custom-call(s32[3]{0:T(128)} %pad_add_fusion.info, f32[96]{0:T(128)} %constant.152.clone.square_z, f32[96]{0:T(128)} %constant.153.clone.decay_z, f32[2,31,2,2,24,384]{5,4,3,2,1,0:T(8,128)} %get-tuple-element.7.s0.s2, f32[2,31,2,2,24,384]{5,4,3,2,1,0:T(8,128)} %get-tuple-element.8.s1.s3, ...), custom_call_target="tpu_custom_call" | custom-call | tf_op jit(solution)/shard_map/pallas_call | solution.py:447
  212.3 15.9 %shard_map.242 = f32[2,48,4608]{2,1,0:T(8,128)} custom-call(s32[3]{0:T(128)} %pad_add_fusion.info, f32[2]{0:T(128)} %maximum_multiply_fusion.weight, f32[3,9216,128]{2,1,0:T(8,128)} %shard_map.240.work, f32[2,31,2,2,24,384]{5,4,3,2,1,0:T(8,128)} %get-tuple-element.7.s0.s2, f32[2,31,2,2,24,384]{5,4,3,2,1,0:T(8,128)} %get-tuple-element.8.s1.s3, ...), custom_call_target="tpu_custom_call" | custom-call | flops 2038431744 | bytes 56623104 | tf_op jit(solution)/shard_map/pallas_call | solution.py:482
  228.7 15.8 %shard_map.244 = f32[2,48,4608]{2,1,0:T(8,128)} custom-call(s32[3]{0:T(128)} %pad_add_fusion.info, f32[2]{0:T(128)} %maximum_multiply_fusion.weight, f32[3,9216,128]{2,1,0:T(8,128)} %shard_map.240.work, f32[2,31,2,2,24,384]{5,4,3,2,1,0:T(8,128)} %get-tuple-element.7.s0.s2, f32[2,31,2,2,24,384]{5,4,3,2,1,0:T(8,128)} %get-tuple-element.8.s1.s3, ...), custom_call_target="tpu_custom_call" | custom-call | flops 2038431744 | bytes 56623104 | tf_op jit(solution)/shard_map/pallas_call | solution.py:482
  244.5 1.5 collective-permute-start.1
  246.0 1.7 dynamic-slice_bitcast_fusion.4
  247.7 15.8 %shard_map.241 = f32[2,48,4608]{2,1,0:T(8,128)} custom-call(s32[3]{0:T(128)} %pad_add_fusion.info, f32[2]{0:T(128)} %maximum_multiply_fusion.weight, f32[3,9216,128]{2,1,0:T(8,128)} %shard_map.240.work, f32[2,31,2,2,24,384]{5,4,3,2,1,0:T(8,128)} %get-tuple-element.7.s0.s2, f32[2,31,2,2,24,384]{5,4,3,2,1,0:T(8,128)} %get-tuple-element.8.s1.s3, ...), custom_call_target="tpu_custom_call" | custom-call | flops 2038431744 | bytes 56623104 | tf_op jit(solution)/shard_map/pallas_call | solution.py:482
  263.6 16.0 %shard_map.243 = f32[2,48,4608]{2,1,0:T(8,128)} custom-call(s32[3]{0:T(128)} %pad_add_fusion.info, f32[2]{0:T(128)} %maximum_multiply_fusion.weight, f32[3,9216,128]{2,1,0:T(8,128)} %shard_map.240.work, f32[2,31,2,2,24,384]{5,4,3,2,1,0:T(8,128)} %get-tuple-element.7.s0.s2, f32[2,31,2,2,24,384]{5,4,3,2,1,0:T(8,128)} %get-tuple-element.8.s1.s3, ...), custom_call_target="tpu_custom_call" | custom-call | flops 2038431744 | bytes 56623104 | tf_op jit(solution)/shard_map/pallas_call | solution.py:482
  279.6 2.9 fusion.3
  282.5 24.6 %collective-permute-done.1 = f32[2,48,4608]{2,1,0:T(8,128)S(1)} collective-permute-done((f32[2,48,4608]{2,1,0:T(8,128)}, f32[2,48,4608]{2,1,0:T(8,128)S(1)}, u32[]{:S(2)}, u32[]{:S(2)}) %collective-permute-start.1) | collective-permute-done | bytes 1769504 | tf_op jit(solution)/shard_map/ppermute | solution.py:519
  307.2 1.5 fusion.2
  308.7 2.8 collective-permute-done.3
  311.4 2.4 fusion.1
  316.1 1.2 multiply_reduce_fusion.2
  317.9 5.9 %psum.7 = f32[3,2]{1,0:T(4,128)S(1)} all-reduce(f32[3,2]{1,0:T(4,128)S(1)} %pad_maximum_fusion.3), channel_id=1, replica_groups=mesh['band'=8,'grid'=4] {'grid'}, use_global_device_ids=true, to_apply=%region_4.5 | all-reduce | flops 6 | bytes 48 | tf_op jit(solution)/shard_map/psum | solution.py:625
  323.8 3.7 %multiply_add_fusion = f32[2,2,24,9216]{3,2,0,1:T(8,128)S(1)} fusion(f32[2]{0:T(128)S(1)} %multiply_bitcast_fusion, f32[2,2,24,9216]{3,2,1,0:T(8,128)S(1)} %copy-done, f32[1,2,24,9216]{3,2,0,1:T(8,128)} %copy-done.6, f32[1,2,24,9216]{3,2,0,1:T(8,128)} %copy-done.5, f32[1,2,24,9216]{3,2,0,1:T(8,128)} %copy-done.3, f32[1,2,24,9216]{3,2,0,1:T(8,128)} %copy-done.1), kind=kLoop, calls=%fused_computation.3 | loop fusion | flops 4423680 | bytes 14155784 | tf_op jit(solution)/shard_map/add | solution.py:627
  327.5 2.0 copy.33
  (33 shorter events, 7.6 us)
Async XLA Ops:
  7.2 3.3 %copy-start = (f32[2,2,24,9216]{3,2,1,0:T(8,128)S(1)}, f32[2,2,24,9216]{3,2,1,0:T(8,128)}, u32[]{:S(2)}) copy-start(f32[2,2,24,9216]{3,2,1,0:T(8,128)} %param.24) | copy-start | bytes 10616836
  10.0 1.2 copy-start.1
  10.0 1.8 copy-start.3
  228.1 51.4 %collective-permute-start = (f32[2,48,4608]{2,1,0:T(8,128)}, f32[2,48,4608]{2,1,0:T(8,128)}, u32[]{:S(2)}, u32[]{:S(2)}) collective-permute-start(f32[2,48,4608]{2,1,0:T(8,128)} %shard_map.242), channel_id=1, source_target_pairs={{0,2},{1,3},{2,0},{3,1},{4,6},{5,7},{6,4},{7,5},{8,10},{9,11},{10,... | collective-permute-start | bytes 5308424 | tf_op jit(solution)/shard_map/ppermute | solution.py:519
  244.5 62.6 %collective-permute-start.1 = (f32[2,48,4608]{2,1,0:T(8,128)}, f32[2,48,4608]{2,1,0:T(8,128)S(1)}, u32[]{:S(2)}, u32[]{:S(2)}) collective-permute-start(f32[2,48,4608]{2,1,0:T(8,128)} %shard_map.244), channel_id=1, source_target_pairs={{0,2},{1,3},{2,0},{3,1},{4,6},{5,7},{6,4},{7,5},{8,10},{9,11},{10,... | collective-permute-start | bytes 5308424 | tf_op jit(solution)/shard_map/ppermute | solution.py:519
  263.6 16.0 %copy-start.9 = (f32[2,48,4608]{2,1,0:T(8,128)S(1)}, f32[2,48,4608]{2,1,0:T(8,128)}, u32[]{:S(2)}) copy-start(f32[2,48,4608]{2,1,0:T(8,128)} %shard_map.241) | copy-start | bytes 5308420
  279.6 27.6 %copy-start.8 = (f32[2,48,4608]{2,1,0:T(8,128)S(1)}, f32[2,48,4608]{2,1,0:T(8,128)}, u32[]{:S(2)}) copy-start(f32[2,48,4608]{2,1,0:T(8,128)} %shard_map.243) | copy-start | bytes 5308420
  282.5 26.2 %collective-permute-start.2 = (f32[2,24,4608]{2,1,0:T(8,128)}, f32[2,24,4608]{2,1,0:T(8,128)}, u32[]{:S(2)}, u32[]{:S(2)}) collective-permute-start(f32[2,24,4608]{2,1,0:T(8,128)} %get-tuple-element.25), channel_id=1, source_target_pairs={{0,1},{1,0},{2,3},{3,2},{4,5},{5,4},{6,7},{7,6},{8,9},{9,8},{10,11... | collective-permute-start | bytes 2654216 | tf_op jit(solution)/shard_map/ppermute | solution.py:519
  308.7 2.8 collective-permute-start.3
  311.4 2.5 copy-start.2
  311.4 3.1 copy-start.4
  311.4 3.3 copy-start.7
  316.1 1.2 copy-start.5
  316.1 1.8 copy-start.6
